TPU v7x, 32 devices: a whole 2x2x4 slice. The times are simulated.
32 devices in a mesh: narrow: 8 (over y, x, core), wide: 4 (over z).
Axes of the slice: x: 2, y: 2, z: 4, core: 2. Of those that a mesh axis runs over, the one named last changes fastest.
Arguments:
- feat_p2: float32 [4, 256, 64, 64], P('wide', 'narrow'), may hold values from -6 to 6
- feat_p3: float32 [4, 256, 32, 32], P('wide', 'narrow'), may hold values from -6 to 6
- feat_p4: float32 [4, 256, 16, 16], P('wide', 'narrow'), may hold values from -6 to 6
- feat_p5: float32 [4, 256, 8, 8], P('wide', 'narrow'), may hold values from -6 to 6
- rois: int32 [2, 4, 512, 4], P(None, 'wide'), may hold values from 0 to 256, as said below
- levels: int32 [2, 4, 512], P(None, 'wide'), may hold values from 0 to 3
- labels: int32 [2, 4, 512], P(None, 'wide'), may hold values from 0 to 80
- sampled: int32 [2, 4, 512], P(None, 'wide'), may hold values from 0 to 1
- targets: float32 [2, 4, 512, 4], P(None, 'wide'), may hold values from -6 to 6
- fc1_w: float32 [2, 12544, 1024], P(None, 'narrow'), may hold values from -0.078125 to 0.078125
- fc1_m: float32 [2, 12544, 1024], P(None, 'narrow'), may hold values from -0.09375 to 0.09375
- fc1_v: float32 [2, 12544, 1024], P(None, 'narrow'), may hold values from 2.4414063e-05 to 0.0001953125
- fc2_w: float32 [2, 1024, 1024], P(None, 'narrow'), may hold values from -0.1875 to 0.1875
- fc2_m: float32 [2, 1024, 1024], P(None, 'narrow'), may hold values from -0.09375 to 0.09375
- fc2_v: float32 [2, 1024, 1024], P(None, 'narrow'), may hold values from 2.4414063e-05 to 0.0001953125
- head_w: float32 [2, 1024, 401], P(None, 'narrow'), may hold values from -0.5 to 0.5
- head_m: float32 [2, 1024, 401], P(None, 'narrow'), may hold values from -0.09375 to 0.09375
- head_v: float32 [2, 1024, 401], P(None, 'narrow'), may hold values from 2.4414063e-05 to 0.0001953125
Outputs:
- loss_parts: float32 [2], replicated
- fc1_new: float32 [2, 12544, 1024], P(None, 'narrow')
- fc1_moment: float32 [2, 12544, 1024], P(None, 'narrow')
- fc1_second: float32 [2, 12544, 1024], P(None, 'narrow')
- fc2_new: float32 [2, 1024, 1024], P(None, 'narrow')
- fc2_moment: float32 [2, 1024, 1024], P(None, 'narrow')
- fc2_second: float32 [2, 1024, 1024], P(None, 'narrow')
- head_new: float32 [2, 1024, 401], P(None, 'narrow')
- head_moment: float32 [2, 1024, 401], P(None, 'narrow')
- head_second: float32 [2, 1024, 401], P(None, 'narrow')
Inputs may be any that keep to these rules, and one draw needn't show every extreme that they name: `rois`: integer boxes inside an image of 256 pixels, at least 4 cells wide on their level.
All inputs are finite; a program needn't handle non-finite values.
Results may differ from a plain program's by a relative error of at most 0.0008.
Values may be sent and summed in bfloat16 or wider, within the bound.
A program may use at most 448 MiB of HBM per device.

v0:
```python
from functools import partial

import jax
import jax.numpy as jnp
from jax import lax
from jax.experimental import pallas as pl
from jax.experimental.pallas import tpu as pltpu
from jax.sharding import PartitionSpec as P

CLASSES = 81
STEP = 5
BETA_ONE = 0.5
BETA_TWO = 0.5
RATE = 0.02
DECAY = 0.01
EPSILON = 1e-08
BINS = 7
CHUNK = 8
STATIC = 5
WINDOW = 24
MORE = 4
SPANS = 17
LANES = 128
MIB = 2**20


def tent(where, cells):
    return 0.5 * sum(jnp.maximum(0.0, 1.0 - jnp.abs(w - cells)) for w in where)


def pool_kernel(channels, side, groups, copies, pick_ref, span_ref, feat_ref, table_ref, *refs):
    out_refs = refs[-7 - copies : -7]
    cols, rows, parts = refs[-7:-5], refs[-5:-3], refs[-3:-1]
    line_ref = refs[-1]
    image = pick_ref[0]
    half = LANES // 2
    offsets = (0.25, 0.75)
    cells = lax.broadcasted_iota(jnp.int32, (side, LANES), 0).astype(jnp.float32)
    bins = lax.broadcasted_iota(jnp.int32, (8, LANES), 0).astype(jnp.float32)

    def at(group):
        return (image * groups + group) * SPANS

    def param(group, k):
        return table_ref[group, k : k + 1, :]

    def weights(group, slot):
        top, x_start, x_step = param(group, 2), param(group, 4), param(group, 5)
        for j in range(BINS):
            where = [jnp.clip(x_start + (j + off) * x_step, 0.0, top) for off in offsets]
            weight = tent(where, cells)
            high = weight.astype(jnp.bfloat16)
            low = (weight - high.astype(jnp.float32)).astype(jnp.bfloat16)
            lanes = pl.ds(j * LANES, LANES)
            cols[slot][0:side, lanes] = high
            cols[slot][side : 2 * side, lanes] = high
            cols[slot][2 * side : 3 * side, lanes] = low
            cols[slot][3 * side : 4 * side, lanes] = low

    def fill(group, slot, row):
        y_start, y_step, top, base = (param(group, k) for k in range(4))
        where = [jnp.clip(y_start + (bins + off) * y_step, 0.0, top) for off in offsets]
        for h in range(CHUNK):
            rows[slot][row + h] = tent(where, (row + h).astype(jnp.float32) - base)
        place = pl.ds(pl.multiple_of(row * channels, channels), CHUNK * channels)
        left = feat_ref[place, :]
        left = jnp.concatenate([left, left], axis=1)
        parts[slot][place, :] = jnp.dot(left, cols[slot][...], preferred_element_type=jnp.float32)

    def rest(group, slot):
        first = span_ref[at(group)] + STATIC * CHUNK

        @pl.loop(0, span_ref[at(group) + 1])
        def _(t):
            fill(group, slot, first + t * CHUNK)

    def block(slot, i, low_row, count):
        accs = None
        for h in range(count):
            start = pl.multiple_of((low_row + h) * channels, channels)
            weight = jnp.broadcast_to(rows[slot][low_row + h, i : i + 1, :], (channels, LANES))
            new = [
                weight * parts[slot][pl.ds(start, channels), j * LANES : (j + 1) * LANES] for j in range(BINS)
            ]
            accs = new if accs is None else [x + y for x, y in zip(accs, new)]
        return accs

    def spot(i, j):
        return pl.ds(i * BINS + j, channels, stride=BINS * BINS)

    def work(group, slot, following):
        for i in range(BINS):
            accs = block(slot, i, span_ref[at(group) + 3 + i], WINDOW)
            for j in range(BINS):
                line_ref[slot, spot(i, j), :] = accs[j]
            if i < STATIC:
                fill(following, 1 - slot, span_ref[at(following)] + i * CHUNK)

        @pl.when(span_ref[at(group) + 2] > 0)
        def _():
            for i in range(BINS):
                low_row = span_ref[at(group) + 3 + i] + WINDOW

                @pl.loop(0, span_ref[at(group) + 3 + BINS + i])
                def _(t):
                    more = block(slot, i, low_row + t * MORE, MORE)
                    for j in range(BINS):
                        line_ref[slot, spot(i, j), :] = line_ref[slot, spot(i, j), :] + more[j]

    step = pl.program_id(0)

    @pl.when(step == 0)
    def _():
        weights(0, 0)
        for i in range(STATIC):
            fill(0, 0, span_ref[at(0)] + i * CHUNK)
        rest(0, 0)

    group = 2 * step
    weights(group + 1, 1)
    work(group, 0, group + 1)
    rest(group + 1, 1)
    following = jnp.minimum(group + 2, groups - 1)
    weights(following, 0)
    work(group + 1, 1, following)
    rest(following, 0)
    a, b = line_ref[0], line_ref[1]
    lanes = lax.broadcasted_iota(jnp.int32, a.shape, 1)
    new = [jnp.where(lanes < half, a, pltpu.roll(b, half, 1)), jnp.where(lanes < half, pltpu.roll(a, half, 1), b)]
    for out_ref in out_refs:
        for p in range(2):
            out_ref[p] = new[p].astype(jnp.bfloat16)


def pool(feat, table, spans, source, image, images, channels, buffer=None):
    depth = feat.shape[2]
    groups = table.shape[1]
    wide = channels * BINS * BINS
    side = depth // 2
    rows = sum(side >> k for k in range(4))
    boxes = groups * LANES // 2
    blocks = groups // 2
    pick = jnp.stack([source, image])
    out_shape = [jax.ShapeDtypeStruct((2, wide, images * boxes), jnp.bfloat16)]
    out_specs = [pl.BlockSpec((2, wide, LANES), lambda s, pick, spans: (0, 0, pick[1] * blocks + s))]
    in_specs = [
        pl.BlockSpec((None, rows * channels, depth), lambda s, pick, spans: (pick[0], 0, 0)),
        pl.BlockSpec((None, groups, 8, LANES), lambda s, pick, spans: (pick[0], 0, 0, 0)),
    ]
    operands = (pick, spans, feat, table)
    aliases = {}
    if buffer is None:
        out_shape.append(jax.ShapeDtypeStruct((2, wide, boxes), jnp.bfloat16))
        out_specs.append(pl.BlockSpec((2, wide, LANES), lambda s, pick, spans: (0, 0, s)))
    else:
        in_specs.append(pl.BlockSpec(memory_space=pl.ANY))
        operands += (buffer,)
        aliases = {4: 0}
    return pl.pallas_call(
        partial(pool_kernel, channels, side, groups, len(out_shape)),
        out_shape=out_shape,
        grid_spec=pltpu.PrefetchScalarGridSpec(
            num_scalar_prefetch=2,
            grid=(blocks,),
            in_specs=in_specs,
            out_specs=out_specs,
            scratch_shapes=[
                pltpu.VMEM((4 * side, BINS * LANES), jnp.bfloat16),
                pltpu.VMEM((4 * side, BINS * LANES), jnp.bfloat16),
                pltpu.VMEM((rows, 8, LANES), jnp.float32),
                pltpu.VMEM((rows, 8, LANES), jnp.float32),
                pltpu.VMEM((rows * channels, BINS * LANES), jnp.float32),
                pltpu.VMEM((rows * channels, BINS * LANES), jnp.float32),
                pltpu.VMEM((2, wide, LANES), jnp.float32),
            ],
        ),
        input_output_aliases=aliases,
        compiler_params=pltpu.CompilerParams(vmem_limit_bytes=44 * MIB),
        cost_estimate=pl.CostEstimate(
            flops=groups * 40 * channels * BINS * LANES * 8 * depth,
            bytes_accessed=80 * MIB,
            transcendentals=0,
        ),
        name="pool_rois",
    )(*operands)


def feature_rows(maps):
    side = maps[0].shape[-1]
    parts = [
        jnp.pad(m.transpose(0, 2, 1, 3), ((0, 0), (0, 0), (0, 0), (0, side - m.shape[-1])))
        for m in maps
    ]
    full = jnp.concatenate(parts, axis=1)
    high = lax.reduce_precision(full, 8, 7)
    low = (full - high).astype(jnp.bfloat16)
    full = jnp.concatenate([high.astype(jnp.bfloat16), low], axis=-1)
    return full.reshape(-1, 2 * side)


def box_order(boxes, levels, side):
    base = 2 * side - 2 * (side >> levels)
    key = ((boxes[..., 1] + boxes[..., 3]) >> levels) + base * 8
    key = key * key.shape[-1] + jnp.arange(key.shape[-1], dtype=jnp.int32)
    return jnp.sum((key[..., :, None] > key[..., None, :]).astype(jnp.int32), axis=-1)


def sort_boxes(boxes, levels, rank):
    count = boxes.shape[1]
    hot = (rank[:, None, :] == jnp.arange(count, dtype=jnp.int32)[:, None]).astype(jnp.bfloat16)
    both = jnp.concatenate([boxes, levels[..., None]], axis=-1).astype(jnp.bfloat16)
    return jnp.einsum("psr,prk->kps", hot, both, preferred_element_type=jnp.float32).astype(jnp.bfloat16)


def box_table(boxes, side):
    images, _, _, count = boxes.shape
    x0, y0, x1, y1, level = (boxes[:, k].astype(jnp.float32) for k in range(5))
    rows = sum(side >> k for k in range(4))
    scale = jnp.where(level < 0.5, 0.25, jnp.where(level < 1.5, 0.125, jnp.where(level < 2.5, 0.0625, 0.03125)))
    height = scale * (4 * side)
    base = 2.0 * side - 2.0 * height
    top = height - 1.0

    def axis(low, high):
        return low * scale - 0.5, ((high - low) * scale) / 7.0

    x_start, x_step = axis(x0, x1)
    y_start, y_step = axis(y0, y1)
    half = LANES // 2
    groups = count // half

    def split(v):
        return v.reshape(v.shape[:-1] + (groups, half))

    lows, highs = [], []
    for i in range(BINS):
        low = base + jnp.floor(jnp.clip(y_start + (i + 0.25) * y_step, 0.0, top))
        high = base + jnp.floor(jnp.clip(y_start + (i + 0.75) * y_step, 0.0, top)) + 1.0
        lows.append(jnp.min(split(low), axis=(1, 3)))
        highs.append(jnp.max(split(jnp.minimum(high, rows - 1.0)), axis=(1, 3)))
    low = jnp.stack(lows, axis=-1).astype(jnp.int32)
    high = jnp.stack(highs, axis=-1).astype(jnp.int32)
    least = jnp.min(low, axis=-1)
    chunks = jnp.maximum((jnp.max(high, axis=-1) - least + CHUNK) // CHUNK, STATIC)
    first = jnp.clip(rows - chunks * CHUNK, 0, least)
    extra = jnp.maximum(high - low + MORE - WINDOW, 0) // MORE
    low = jnp.minimum(low, (first + chunks * CHUNK)[..., None] - WINDOW - MORE * extra)
    heads = jnp.stack([first, chunks - STATIC, jnp.max(extra, axis=-1)], axis=-1)
    spans = jnp.concatenate([heads, low, extra], axis=-1).reshape(-1)
    zero = jnp.zeros_like(base)
    table = jnp.stack([split(v) for v in (y_start, y_step, top, base, x_start, x_step, zero, zero)])
    return table.transpose(1, 3, 0, 2, 4).reshape(images, groups, 8, LANES), spans


def adamw(weight, moment, second, grad):
    moment = BETA_ONE * moment + (1.0 - BETA_ONE) * grad
    second = BETA_TWO * second + (1.0 - BETA_TWO) * grad * grad
    fixed_m = moment / (1.0 - BETA_ONE**STEP)
    fixed_v = second / (1.0 - BETA_TWO**STEP)
    weight = weight - RATE * (fixed_m / (jnp.sqrt(fixed_v) + EPSILON) + DECAY * weight)
    return (weight, moment, second)


def update_kernel(pooled_ref, back_ref, w_ref, m_ref, v_ref, *outs):
    grad = jnp.dot(pooled_ref[...], back_ref[...], preferred_element_type=jnp.float32)
    new = adamw(w_ref[...], m_ref[...], v_ref[...], grad)
    for ref, value in zip(outs, new):
        ref[...] = value


def update_first(pooled, back, weight, moment, second):
    passes, wide, hidden = weight.shape
    boxes = pooled.shape[2]
    block = wide // BINS
    big = pl.BlockSpec((None, block, hidden), lambda p, b: (p, b, 0))
    return pl.pallas_call(
        update_kernel,
        out_shape=[jax.ShapeDtypeStruct(weight.shape, jnp.float32)] * 3,
        grid=(passes, BINS),
        in_specs=[
            pl.BlockSpec((None, block, boxes), lambda p, b: (p, b, 0)),
            pl.BlockSpec((None, boxes, hidden), lambda p, b: (p, 0, 0)),
            big,
            big,
            big,
        ],
        out_specs=[big] * 3,
        compiler_params=pltpu.CompilerParams(vmem_limit_bytes=56 * MIB),
        cost_estimate=pl.CostEstimate(
            flops=2 * passes * wide * hidden * boxes,
            bytes_accessed=passes * wide * hidden * 24 + passes * boxes * (wide + hidden) * 2,
            transcendentals=passes * wide * hidden,
        ),
        name="update_first",
    )(pooled, back, weight, moment, second)


def loss_and_slope(logits, box, count):
    place = lax.broadcasted_iota(jnp.int32, logits.shape, 1)
    is_class = place < CLASSES
    label = box[:, 0:1].astype(jnp.int32)
    weight = box[:, 1:2]
    top = jnp.max(jnp.where(is_class, logits, -jnp.inf), axis=1, keepdims=True)
    grown = jnp.where(is_class, jnp.exp(jnp.where(is_class, logits - top, 0.0)), 0.0)
    norm = jnp.sum(grown, axis=1, keepdims=True)
    hot = place == label
    picked = jnp.sum(jnp.where(hot, logits, 0.0), axis=1, keepdims=True)
    fore = jnp.where(label > 0, weight, 0.0)
    rows = weight * (top + jnp.log(norm) - picked)
    slope = weight * (grown / norm - jnp.where(hot, 1.0, 0.0))
    offset = place - (CLASSES + 4 * (label - 1))
    for k in range(4):
        mask = (offset == k) & (place >= CLASSES)
        chosen = jnp.sum(jnp.where(mask, logits, 0.0), axis=1, keepdims=True)
        differ = fore * (chosen - box[:, 2 + k : 3 + k])
        near = jnp.abs(differ)
        rows += jnp.where(near < 1.0, 0.5 * differ * differ, near - 0.5) * fore
        slope = jnp.where(mask, fore * jnp.clip(differ, -1.0, 1.0), slope)
    return rows, slope / count


def sigmoid(value):
    return 1.0 / (1.0 + jnp.exp(-value))


def head_kernel(
    images, parts, mine,
    part_ref, weight_ref, box_ref, count_ref,
    back_ref, grad_ref,
    sums, landed, own, counts, turned, cols, kept,
    rs_send, rs_recv, ag_send, ag_recv, up_send, up_recv, down_send, down_recv, own_sem,
    count_send, count_recv, col_send, col_recv, kept_send, kept_recv,
):
    me = lax.axis_index("narrow")
    level = lax.axis_index("wide")
    bits = parts.bit_length() - 1
    turn = [(1 - 2 * ((me // 2**k) % 2)) * 2**k for k in range(bits)]

    def peer(mask):
        return me + sum((turn[k] for k in range(bits) if mask >> k & 1), 0)

    links = list(range(1, bits))
    orders = [links, links[::-1]]

    barrier = pltpu.get_barrier_semaphore()
    for mask in range(1, parts):
        pl.semaphore_signal(barrier, inc=1, device_id={"narrow": peer(mask)})
    for k in range(1, images):
        pl.semaphore_signal(barrier, inc=1, device_id={"wide": lax.rem(level + k, images)})
    pl.semaphore_wait(barrier, parts + images - 2)

    counting = []
    for k in range(1, images):
        counting.append(
            pltpu.make_async_remote_copy(
                src_ref=count_ref,
                dst_ref=counts.at[k],
                send_sem=count_send.at[k],
                recv_sem=count_recv.at[k],
                device_id={"wide": lax.rem(level + k, images)},
            )
        )

    def scatter(p, mask, bit, source):
        return pltpu.make_async_remote_copy(
            src_ref=source,
            dst_ref=landed.at[p, mask],
            send_sem=rs_send.at[p, mask],
            recv_sem=rs_recv.at[p, mask],
            device_id={"narrow": peer(1 << bit)},
        )

    def part_at(p, mask):
        return part_ref.at[p, pl.ds(pl.multiple_of(peer(mask) * mine, mine), mine), :]

    copies = {}
    for p in range(2):
        for mask in range(1, parts, 2):
            copies[p, mask] = scatter(p, mask, 0, part_at(p, mask))
            copies[p, mask].start()

    def stage(p, at):
        order = [0] + orders[p]
        bit = order[at - 1]
        seen = sum(1 << b for b in order[:at])
        for mask in range(parts):
            if mask & seen:
                continue
            copies[p, mask | 1 << bit].wait_recv()
            if at == 1:
                have = part_ref[p, pl.ds(pl.multiple_of(peer(mask) * mine, mine), mine), :]
            else:
                have = sums[p, mask]
            sums[p, mask] = have + landed[p, mask | 1 << bit]
            if at < bits and mask >> order[at] & 1:
                copies[p, mask] = scatter(p, mask, order[at], sums.at[p, mask])
                copies[p, mask].start()

    for copy in counting:
        copy.start()
    for at in range(1, bits):
        for p in range(2):
            stage(p, at)

    def rows(p, image, mask):
        place = (image * parts + peer(mask)) * mine
        return back_ref.at[p, pl.ds(pl.multiple_of(place, mine), mine), :]

    def hop(p, d, up, source=None):
        image = level - d if up else level + d
        spot = rows(p, image, 0)
        return pltpu.make_async_remote_copy(
            src_ref=spot if source is None else source,
            dst_ref=spot,
            send_sem=(up_send if up else down_send).at[p, d],
            recv_sem=(up_recv if up else down_recv).at[p, d],
            device_id={"wide": level + 1 if up else level - 1},
        )

    def came(p, d, up):
        image = level - d if up else level + d
        spot = rows(p, image, 0)
        pltpu.make_async_remote_copy(
            src_ref=spot, dst_ref=spot, send_sem=(up_send if up else down_send).at[p, d],
            recv_sem=(up_recv if up else down_recv).at[p, d - 1],
            device_id={"wide": level - 1 if up else level + 1},
        ).wait_recv()

    steps = [orders[p] + [0] for p in range(2)]

    def masks_before(p, at):
        seen = sum(1 << b for b in steps[p][:at])
        return [m for m in range(parts) if not m & ~seen]

    def doubling(spot, send, recv):
        def spread(p, key, mask, bit, source=None):
            there = mask | 1 << bit
            return pltpu.make_async_remote_copy(
                src_ref=spot(p, key, mask) if source is None else source,
                dst_ref=spot(p, key, mask),
                send_sem=send.at[p, key, there],
                recv_sem=recv.at[p, key, there],
                device_id={"narrow": peer(1 << bit)},
            )

        def arrive(p, key, at):
            for m in masks_before(p, at):
                there = m | 1 << steps[p][at]
                pltpu.make_async_remote_copy(
                    src_ref=spot(p, key, there),
                    dst_ref=spot(p, key, there),
                    send_sem=send.at[p, key, there],
                    recv_sem=recv.at[p, key, there],
                    device_id={"narrow": peer(1)},
                ).wait_recv()

        def advance(p, key, at, source=None):
            if at:
                arrive(p, key, at - 1)
            for m in masks_before(p, at):
                spread(p, key, m, steps[p][at], source if m == 0 else None).start()

        def sent(p, key):
            for at in range(bits):
                for m in masks_before(p, at):
                    spread(p, key, m, steps[p][at]).wait_send()

        return advance, arrive, sent

    advance, arrive, sent = doubling(rows, ag_send, ag_recv)
    advance_kept, arrive_kept, sent_kept = doubling(
        lambda p, key, mask: kept.at[p, peer(mask)], kept_send, kept_recv
    )

    def finish(p, image):
        arrive(p, image, bits - 1)
        sent(p, image)

    span = grad_ref.shape[1]

    def columns(p, mask):
        return turned.at[p, :, pl.ds(pl.multiple_of(peer(mask) * span, span), span), :]

    def hand(p, mask):
        return pltpu.make_async_remote_copy(
            src_ref=columns(p, mask),
            dst_ref=cols.at[p, mask],
            send_sem=col_send.at[p, mask],
            recv_sem=col_recv.at[p, mask],
            device_id={"narrow": peer(mask)},
        )

    for copy in counting:
        copy.wait_recv()
    count = count_ref[0:1, 0:1] + sum(counts[k, 0:1, 0:1] for k in range(1, images))
    hidden = part_ref.shape[2]
    for p in range(2):
        stage(p, bits)
        pre1 = sums[p, 0]
        sig1 = sigmoid(pre1)
        hid1 = (pre1 * sig1).astype(jnp.bfloat16)
        pre2 = jnp.dot(hid1, weight_ref[p, :, :hidden], preferred_element_type=jnp.float32)
        sig2 = sigmoid(pre2)
        hid2 = (pre2 * sig2).astype(jnp.bfloat16)
        logits = jnp.dot(hid2, weight_ref[p, :, hidden:], preferred_element_type=jnp.float32)
        loss, slope = loss_and_slope(logits, box_ref[p], count)
        back_z = slope.astype(jnp.bfloat16)
        across = (((1,), (1,)), ((), ()))
        back_h2 = lax.dot_general(back_z, weight_ref[p, :, hidden:], across, preferred_element_type=jnp.float32)
        back_p2 = (back_h2 * (sig2 * (1.0 + pre2 * (1.0 - sig2)))).astype(jnp.bfloat16)
        back_h1 = lax.dot_general(back_p2, weight_ref[p, :, :hidden], across, preferred_element_type=jnp.float32)
        own[p] = (back_h1 * (sig1 * (1.0 + pre1 * (1.0 - sig1)))).astype(jnp.bfloat16)

        @pl.when(level < images - 1)
        def _():
            hop(p, 0, True, own.at[p]).start()

        @pl.when(level > 0)
        def _():
            hop(p, 0, False, own.at[p]).start()

        advance(p, level, 0, own.at[p])
        pltpu.make_async_copy(own.at[p], rows(p, level, 0), own_sem.at[p]).start()
        place = lax.broadcasted_iota(jnp.int32, (mine, LANES), 1)
        losses = jnp.zeros((mine, LANES), jnp.float32)
        for k in range(3):
            near = loss.astype(jnp.bfloat16).astype(jnp.float32)
            losses = jnp.where(place == k, near, losses)
            loss = loss - near
        at = 0
        for value in (back_p2, back_z, losses.astype(jnp.bfloat16)):
            kept[p, me, :, at : at + value.shape[1]] = value
            at += value.shape[1]
        advance_kept(p, 0, 0)
        turned[p, 0] = hid1.T
        turned[p, 1] = hid2.T
        for mask in range(1, parts):
            hand(p, mask).start()
    for p in range(2):
        pltpu.make_async_copy(own.at[p], rows(p, level, 0), own_sem.at[p]).wait()

    def each_side(d, do):
        @pl.when(level >= d)
        def _():
            do(level - d, True)

        @pl.when(level + d < images)
        def _():
            do(level + d, False)

    def enter(d):
        def do(image, up):
            for p in range(2):
                came(p, d, up)

                @pl.when((level < images - 1) if up else (level > 0))
                def _():
                    hop(p, d, up).start()

                advance(p, image, 0)

        each_side(d, do)

    def go_on(d, at):
        if d == 0:
            for p in range(2):
                advance(p, level, at)
                advance_kept(p, 0, at)
        else:

            def do(image, up):
                for p in range(2):
                    advance(p, image, at)

            each_side(d, do)

    for tick in range(1, images + bits - 1):
        for d in range(images):
            at = tick - d
            if at == 0:
                enter(d)
            elif 0 < at < bits:
                go_on(d, at)

    loss = jnp.zeros((1, 1), jnp.float32)
    for p in range(2):
        arrive_kept(p, 0, bits - 1)
        two, head = [], []
        for mask in range(parts):
            if mask:
                hand(p, mask).wait_recv()
            mine_ref = cols.at[p, mask] if mask else columns(p, 0)
            slopes = kept.at[p, peer(mask)]
            two.append(jnp.dot(mine_ref[0], slopes[:, :hidden], preferred_element_type=jnp.float32))
            head.append(jnp.dot(mine_ref[1], slopes[:, hidden:-LANES], preferred_element_type=jnp.float32))
            loss += jnp.sum(slopes[:, -LANES:].astype(jnp.float32), keepdims=True)
        grad_ref[p, :, :hidden] = sum(two)
        grad_ref[p, :, hidden:] = sum(head)
    corner = grad_ref[0, 0:8, grad_ref.shape[2] - LANES :]
    place = [lax.broadcasted_iota(jnp.int32, corner.shape, k) for k in range(2)]
    corner = jnp.where((place[0] == 0) & (place[1] == LANES - 1), loss, corner)
    grad_ref[0, 0:8, grad_ref.shape[2] - LANES :] = corner

    for p in range(2):
        finish(p, level)
        sent_kept(p, 0)
        for mask in range(1, parts):
            hand(p, mask).wait_send()

        @pl.when(level < images - 1)
        def _():
            hop(p, 0, True).wait_send()

        @pl.when(level > 0)
        def _():
            hop(p, 0, False).wait_send()

    for d in range(1, images):

        def do(image, up):
            for p in range(2):
                finish(p, image)

                @pl.when((level < images - 1) if up else (level > 0))
                def _():
                    hop(p, d, up).wait_send()

        each_side(d, do)
    for p in range(2):
        for mask in range(1, parts):
            copies[p, mask].wait_send()
    for copy in counting:
        copy.wait_send()


def head_step(part, weight, box, count, images, parts):
    passes, boxes, hidden = part.shape
    mine = boxes // parts
    outs = weight.shape[2] - hidden
    span = hidden // parts
    low = jnp.bfloat16
    vmem = pl.BlockSpec(memory_space=pltpu.VMEM)
    dma = pltpu.SemaphoreType.DMA
    return pl.pallas_call(
        partial(head_kernel, images, parts, mine),
        out_shape=[
            jax.ShapeDtypeStruct((passes, images * boxes, hidden), low),
            jax.ShapeDtypeStruct((passes, span, hidden + outs), jnp.float32),
        ],
        in_specs=[vmem] * 4,
        out_specs=[pl.BlockSpec(memory_space=pl.ANY), vmem],
        scratch_shapes=[
            pltpu.VMEM((passes, parts, mine, hidden), jnp.float32),
            pltpu.VMEM((passes, parts, mine, hidden), jnp.float32),
            pltpu.VMEM((passes, mine, hidden), low),
            pltpu.VMEM((images, 8, LANES), jnp.float32),
            pltpu.VMEM((passes, 2, hidden, mine), low),
            pltpu.VMEM((passes, parts, 2, span, mine), low),
            pltpu.VMEM((passes, parts, mine, hidden + outs + LANES), low),
            dma((passes, parts)),
            dma((passes, parts)),
            dma((passes, images, parts)),
            dma((passes, images, parts)),
            dma((passes, images)),
            dma((passes, images)),
            dma((passes, images)),
            dma((passes, images)),
            dma((passes,)),
            dma((images,)),
            dma((images,)),
            dma((passes, parts)),
            dma((passes, parts)),
            dma((passes, 1, parts)),
            dma((passes, 1, parts)),
        ],
        compiler_params=pltpu.CompilerParams(
            vmem_limit_bytes=48 * MIB, collective_id=0, has_side_effects=True
        ),
        cost_estimate=pl.CostEstimate(
            flops=8 * passes * mine * hidden * (hidden + outs),
            bytes_accessed=100 * MIB,
            transcendentals=4 * passes * mine * hidden,
        ),
        name="head_step",
    )(part, weight, box, count)


def small_kernel(grad_ref, *refs):
    at = 0
    for k in range(2):
        weight, moment, second = (r[...] for r in refs[3 * k : 3 * k + 3])
        new = adamw(weight, moment, second, grad_ref[:, at : at + weight.shape[1]])
        for ref, value in zip(refs[6 + 3 * k : 9 + 3 * k], new):
            ref[...] = value
        at += weight.shape[1]


def update_small(grad, *arrays):
    def spec(x):
        return pl.BlockSpec((None,) + x.shape[1:], lambda p: (p, 0, 0))

    return pl.pallas_call(
        small_kernel,
        out_shape=[jax.ShapeDtypeStruct(x.shape, jnp.float32) for x in arrays],
        grid=(grad.shape[0],),
        in_specs=[spec(x) for x in (grad,) + arrays],
        out_specs=[spec(x) for x in arrays],
        compiler_params=pltpu.CompilerParams(vmem_limit_bytes=24 * MIB),
        name="update_small",
    )(grad, *arrays)


def per_device(
    feat_p2, feat_p3, feat_p4, feat_p5, rois, levels, labels, sampled, targets,
    fc1_w, fc1_m, fc1_v, fc2_w, fc2_m, fc2_v, head_w, head_m, head_v,
):
    side = feat_p2.shape[-1]
    channels = feat_p2.shape[1]
    boxes = rois.shape[2]
    images = lax.axis_size("wide")
    mine = boxes // lax.axis_size("narrow")
    first = lax.axis_index("narrow") * mine
    level = lax.axis_index("wide").astype(jnp.int32)
    parts = lax.axis_size("narrow")
    hidden = fc2_w.shape[2]
    outs = head_w.shape[2]
    zero = jnp.zeros((), jnp.int32)
    rank = box_order(rois[:, 0], levels[:, 0], side)
    ordered = sort_boxes(rois[:, 0], levels[:, 0], rank)
    feat = feature_rows((feat_p2, feat_p3, feat_p4, feat_p5))
    height = feat.shape[0]
    flags = sampled[:, 0].astype(jnp.bfloat16).reshape(1, 2, boxes)
    both = jnp.concatenate([feat, jnp.concatenate([ordered, flags]).reshape(-1, LANES)])
    weight = jnp.concatenate([fc2_w, jnp.pad(head_w, ((0, 0), (0, 0), (0, -outs % LANES)))], axis=2)
    weight = lax.all_gather(weight.astype(jnp.bfloat16), "narrow", axis=1, tiled=True)
    counted = jnp.sum(sampled).astype(jnp.float32)
    table, spans = box_table(ordered[None], side)
    pooled, own = pool(feat[None], table, spans, zero, level, images, channels)
    w1 = fc1_w.astype(jnp.bfloat16)
    part = lax.dot_general(own, w1, (((1,), (1,)), ((0,), (0,))), preferred_element_type=jnp.float32)
    both, weight, part = lax.optimization_barrier((both, weight, part))
    feats = lax.all_gather(both, "wide", axis=0)
    hot = rank[:, None, :] == first + jnp.arange(mine, dtype=jnp.int32)[:, None]

    def pick(values):
        return jnp.sum(jnp.where(hot, values[:, 0].astype(jnp.float32)[:, None, :], 0), axis=-1)

    box = [pick(labels), pick(sampled)] + [pick(targets[..., k]) for k in range(4)]
    box = jnp.pad(jnp.stack(box, axis=-1), ((0, 0), (0, 0), (0, LANES - 6)))
    back, grad = head_step(part, weight, box, jnp.full((8, LANES), counted), images, parts)
    grad = lax.psum_scatter(grad, "wide", scatter_dimension=1, tiled=True)

    tails = feats[:, height:].reshape(images, 6, 2, boxes)
    count = jnp.sum(tails[:, 5].astype(jnp.float32))
    tables, all_spans = box_table(tails[:, :5], side)
    turn = [lax.rem(level + k, images) for k in range(1, images)]
    for k in range(images - 1):
        pooled = pool(feats, tables, all_spans, turn[k], turn[k], images, channels, pooled)[0]
        if k == max(images - 3, 0):
            grad, pooled = lax.optimization_barrier((grad, pooled))
            grad = lax.all_gather(grad, "wide", axis=1, tiled=True)
    new1 = update_first(pooled, back, fc1_w, fc1_m, fc1_v)
    grad, new1 = lax.optimization_barrier((grad, new1))
    total = grad[0, 0, -1]
    new = update_small(grad, fc2_w, fc2_m, fc2_v, head_w, head_m, head_v)
    return (jnp.stack([total, count]),) + tuple(new1) + tuple(new)


def solution(mesh):
    maps = P("wide", "narrow", None, None)
    rows = P(None, "narrow", None)
    box = P(None, "wide", None)
    coords = P(None, "wide", None, None)
    return jax.shard_map(
        per_device,
        mesh=mesh,
        in_specs=(maps,) * 4 + (coords, box, box, box, coords) + (rows,) * 9,
        out_specs=(P(),) + (rows,) * 9,
        check_vma=False,
    )
```

profile of v0, /device:TPU:0, one launch (start us, length us, event | category | flops | bytes accessed | tf_op | source)
XLA Modules:
  0.0 314.7 jit_solution(4615955955646684666)
XLA Ops:
  7.2 1.3 convert.24
  8.5 1.2 convert.25
  9.7 0.2 copy.202
  9.9 0.9 fusion.10
  11.0 0.4 convert_reduce_fusion
  11.5 0.5 fusion.8
  12.0 0.1 minimum_reduce_fusion.7
  12.3 0.1 reduce_min.187
  12.4 0.1 reduce_min.190
  12.6 0.1 reduce_min.196
  12.8 0.1 reduce_min.202
  13.0 0.1 reduce_min.205
  13.2 0.1 reduce_min.211
  13.4 0.1 reduce_min.217
  13.6 0.1 reduce_max.203
  13.7 0.1 reduce_max.209
  13.9 0.1 reduce_max.212
  14.1 0.1 reduce_max.218
  14.3 0.1 reduce_max.224
  14.5 0.1 reduce_max.227
  14.7 0.1 reduce_max.233
  16.2 0.2 copy.255
  16.4 0.1 copy.256
  16.5 0.1 select_maximum_fusion
  16.7 0.4 copy.200
  17.1 0.3 copy-done.19
  17.4 0.6 fusion.45
  18.1 0.3 reduce-precision_convert_fusion
  18.4 0.5 pad_maximum_fusion.1.feat_ref
  19.0 0.3 reduce-precision_convert_fusion.1
  19.3 1.5 pad_maximum_fusion
  20.8 22.9 %pool_rois.4 = (bf16[2,1568,2048]{2,1,0:T(8,128)(2,1)}, bf16[2,1568,512]{2,1,0:T(8,128)(2,1)S(1)}) custom-call(s32[2]{0:T(128)S(1)} %pad_add_fusion.pick_ref, s32[136]{0:T(256)S(1)} %reshape.1645.span_ref, bf16[1,3840,128]{2,1,0:T(8,128)(2,1)S(1)} %pad_maximum_fusion.1.feat_ref, f32[1,8,8,128]{3,2,1,0:T(8,128)S(1)} %reshape.1646.table_ref), custom_call_target="tpu_custom_call" | custom-call | flops 9395240960 | bytes 83886080 | tf_op jit(solution)/shard_map/pool_rois/pallas_call | solution.py:159
  43.7 10.3 %fusion.part_ref = f32[2,512,1024]{2,1,0:T(8,128)} fusion(bf16[2,1568,512]{2,1,0:T(8,128)(2,1)S(1)} %get-tuple-element.32, f32[2,1568,1024]{2,1,0:T(8,128)} %w_ref.1), kind=kOutput, calls=%fused_computation | convolution fusion | flops 3291545600 | bytes 20250624 | tf_op jit(solution)/shard_map/dot_general | solution.py:740
  54.0 5.3 %all-gather.5.cloned.1.call-done.weight_ref = bf16[2,1024,1536]{2,1,0:T(8,128)(2,1)} async-done(((bf16[2,128,1536]{2,1,0:T(8,128)(2,1)}), bf16[2,1024,1536]{2,1,0:T(8,128)(2,1)}) %all-gather.5.cloned.1.call-update) | async-done | bytes 6291472 | tf_op jit(solution)/shard_map/all_gather | solution.py:735
  59.3 0.3 reduce-scatter.2.cloned.1.call-start
  59.8 0.3 fusion.16
  61.1 2.2 copy-done
  63.3 109.0 %head_step.1 = (bf16[2,2048,1024]{2,1,0:T(8,128)(2,1)}, f32[2,128,1536]{2,1,0:T(8,128)}) custom-call(f32[2,512,1024]{2,1,0:T(8,128)S(1)} %copy-done, bf16[2,1024,1536]{2,1,0:T(8,128)(2,1)} %all-gather.5.cloned.1.call-done.weight_ref, f32[2,64,128]{2,1,0:T(8,128)S(1)} %pad.25.box_ref, f32[8,128]{1,0:T(8,128)S(1)} %broadcast_in_dim.124.count_ref), custom_call_target="tpu_custom_call" | custom-call | flops 1610612736 | bytes 104857600 | tf_op jit(solution)/shard_map/head_step/pallas_call | solution.py:644
  172.3 0.5 all-gather.7.cloned.1.call-start
  172.8 0.8 slice.89
  173.7 0.2 minimum_reduce_fusion
  177.4 0.2 reshape.1649.table_ref
  178.2 2.1 copy-done.7
  180.3 22.2 %pool_rois.5.refs_0_ = bf16[2,1568,2048]{2,1,0:T(8,128)(2,1)} custom-call(s32[2]{0:T(128)S(1)} %pad_add_fusion.2.pick_ref, s32[544]{0:T(1024)S(1)} %reshape.1648.span_ref, bf16[4,3888,128]{2,1,0:T(8,128)(2,1)S(1)} %bitcast.192, f32[4,8,8,128]{3,2,1,0:T(8,128)S(1)} %reshape.1649.table_ref, ...), custom_call_target="tpu_custom_call", output_to_operand_aliasing={{}: (4, {})} | custom-call | flops 9395240960 | bytes 83886080 | tf_op jit(solution)/shard_map/pool_rois/pallas_call | solution.py:159
  202.5 22.5 %pool_rois.6.refs_0_ = bf16[2,1568,2048]{2,1,0:T(8,128)(2,1)} custom-call(s32[2]{0:T(128)S(1)} %pad_add_fusion.1.pick_ref, s32[544]{0:T(1024)S(1)} %reshape.1648.span_ref, bf16[4,3888,128]{2,1,0:T(8,128)(2,1)S(1)} %bitcast.193, f32[4,8,8,128]{3,2,1,0:T(8,128)S(1)} %reshape.1649.table_ref, ...), custom_call_target="tpu_custom_call", output_to_operand_aliasing={{}: (4, {})} | custom-call | flops 9395240960 | bytes 83886080 | tf_op jit(solution)/shard_map/pool_rois/pallas_call | solution.py:159
  225.1 0.2 copy.235.refs_3_
  225.3 0.2 copy.236.refs_4_
  225.5 0.5 copy-done.13
  226.0 0.2 copy.237.refs_5_
  226.3 0.6 convert_reduce_fusion.1
  227.0 2.1 copy-done.8
  229.1 22.6 %pool_rois.7.pooled_ref = bf16[2,1568,2048]{2,1,0:T(8,128)(2,1)} custom-call(s32[2]{0:T(128)S(1)} %pad_add_fusion.3.pick_ref, s32[544]{0:T(1024)S(1)} %reshape.1648.span_ref, bf16[4,3888,128]{2,1,0:T(8,128)(2,1)S(1)} %bitcast.194, f32[4,8,8,128]{3,2,1,0:T(8,128)S(1)} %reshape.1649.table_ref, ...), custom_call_target="tpu_custom_call", output_to_operand_aliasing={{}: (4, {})} | custom-call | flops 9395240960 | bytes 83886080 | tf_op jit(solution)/shard_map/pool_rois/pallas_call | solution.py:159
  251.7 40.4 %update_first.1 = (f32[2,1568,1024]{2,1,0:T(8,128)}, f32[2,1568,1024]{2,1,0:T(8,128)}, f32[2,1568,1024]{2,1,0:T(8,128)}) custom-call(bf16[2,1568,2048]{2,1,0:T(8,128)(2,1)} %pool_rois.7.pooled_ref, bf16[2,2048,1024]{2,1,0:T(8,128)(2,1)} %get-tuple-element.40.back_ref, f32[2,1568,1024]{2,1,0:T(8,128)} %w_ref.1, f32[2,1568,1024]{2,1,0:T(8,128)} %m_ref.1, ...), custom_call_target="tpu_custom_call" | custom-call | flops 13153337344 | bytes 98304000 | tf_op jit(solution)/shard_map/update_first/pallas_call | solution.py:276
  292.1 1.3 slice.80
  293.4 1.4 copy-done.2
  294.8 1.2 copy-done.3
  296.0 1.2 copy-done.4
  297.3 2.3 update_small.1
  299.6 0.8 copy-done.5
  300.4 0.8 copy-done.6
  301.2 2.0 copy.238
  303.2 2.0 copy.239
  305.2 1.0 copy.240
  306.1 1.9 pad_maximum_fusion.3
  (188 shorter events, 7.3 us)
Async XLA Ops:
  7.2 52.1 %all-gather.5.cloned.1.call-start = ((), (), s32[]{:S(2)}) async-start(), calls=%async_computation.1 | async-start | bytes 7077888 | tf_op jit(solution)/shard_map/all_gather | solution.py:735
  8.5 2.4 copy-start.15
  8.5 2.4 copy-start.18
  9.9 6.3 %copy-start.14 = (f32[1,32,16,16]{1,3,2,0:T(8,128)S(1)}, f32[1,32,16,16]{1,3,2,0:T(8,128)}, u32[]{:S(2)}) copy-start(f32[1,32,16,16]{1,3,2,0:T(8,128)} %param.20) | copy-start | bytes 98308
  9.9 6.5 %copy-start.16 = (f32[1,32,8,8]{1,3,2,0:T(8,128)S(1)}, f32[1,32,8,8]{1,3,2,0:T(8,128)}, u32[]{:S(2)}) copy-start(f32[1,32,8,8]{1,3,2,0:T(8,128)} %param.21) | copy-start | bytes 24580
  9.9 6.6 %copy-start.10 = (f32[1,32,64,64]{3,2,1,0:T(8,128)S(1)}, f32[1,32,64,64]{3,2,1,0:T(8,128)}, u32[]{:S(2)}) copy-start(f32[1,32,64,64]{3,2,1,0:T(8,128)} %param.18) | copy-start | bytes 1572868
  9.9 6.6 %copy-start.11 = (f32[1,32,32,32]{3,2,1,0:T(8,128)S(1)}, f32[1,32,32,32]{3,2,1,0:T(8,128)}, u32[]{:S(2)}) copy-start(f32[1,32,32,32]{3,2,1,0:T(8,128)} %param.19) | copy-start | bytes 393220
  10.9 161.9 %all-gather.9.cloned.1.call-start = ((), (), s32[]{:S(2)}) async-start(), calls=%async_computation.4 | async-start | bytes 4976640 | tf_op jit(solution)/shard_map/all_gather | solution.py:742
  16.7 0.7 copy-start.19
  43.7 16.0 %copy-start.20 = (s32[2,1,512]{2,1,0:T(1,128)S(1)}, s32[2,1,512]{2,1,0:T(1,128)}, u32[]{:S(2)}) copy-start(s32[2,1,512]{2,1,0:T(1,128)} %param.24) | copy-start | bytes 12292
  43.7 16.0 %copy-start.17 = (f32[2,1,512,4]{2,3,1,0:T(4,128)S(1)}, f32[2,1,512,4]{2,3,1,0:T(4,128)}, u32[]{:S(2)}) copy-start(f32[2,1,512,4]{2,3,1,0:T(4,128)} %param.26) | copy-start | bytes 49156
  59.3 165.7 %reduce-scatter.2.cloned.1.call-start = ((), (), s32[]{:S(2)}) async-start(), calls=%async_computation.2 | async-start | bytes 1966080 | tf_op jit(solution)/shard_map/reduce_scatter | solution.py:751
  61.1 2.2 copy-start
  172.3 119.8 %all-gather.7.cloned.1.call-start = ((), (), s32[]{:S(2)}) async-start(), calls=%async_computation.3 | async-start | bytes 1966080 | tf_op jit(solution)/shard_map/all_gather | solution.py:761
  178.2 2.1 copy-start.7
  202.5 22.5 %copy-start.9 = (f32[2,128,401]{1,0,2:T(2,128)S(1)}, f32[2,128,401]{1,0,2:T(2,128)}, u32[]{:S(2)}) copy-start(f32[2,128,401]{1,0,2:T(2,128)} %param.33) | copy-start | bytes 1231876
  202.5 22.8 %copy-start.12 = (f32[2,128,401]{1,0,2:T(2,128)S(1)}, f32[2,128,401]{1,0,2:T(2,128)}, u32[]{:S(2)}) copy-start(f32[2,128,401]{1,0,2:T(2,128)} %param.34) | copy-start | bytes 1231876
  225.0 1.0 copy-start.13
  227.0 2.1 copy-start.8
  251.7 41.7 %copy-start.1 = (f32[2,128,1024]{2,1,0:T(8,128)S(1)}, f32[2,128,1024]{2,1,0:T(8,128)}, u32[]{:S(2)}) copy-start(f32[2,128,1024]{2,1,0:T(8,128)} %refs_0_.1) | copy-start | bytes 3145732
  293.4 1.4 copy-start.2
  294.8 1.2 copy-start.3
  296.0 1.2 copy-start.4
  299.6 0.8 copy-start.5
  300.4 0.8 copy-start.6
Sparse Core Ops, SparseCore 0:
  11.0 48.2 all-gather.4
  61.5 88.6 all-gather.8
  172.4 34.5 reduce-scatter.1
  225.2 36.2 all-gather.6
where the time goes:
time: 320 us; the launch traced here: 315 us
  Pallas kernels  242 us (76%)
  local copies, waits for them, and re-layouts  26.5 us (8%)
  between operations  15.3 us (5%)
  other arithmetic  14 us (4%)
  matrix products  10.8 us (3%)
  waiting for transfers between devices  5.42 us (2%)
    pallas_call x1, Pallas kernels, head_step(): pl.pallas_call(partial(head_kernel, images, parts, mine), out_shape=[jax....  109 us
    pallas_call x4, Pallas kernels, pool(): pl.pallas_call(partial(pool_kernel, channels, side, groups, len(out_shape...  90.1 us
    pallas_call x1, Pallas kernels, update_first(): pl.pallas_call(update_kernel, out_shape=[jax.ShapeDtypeStruct(weight.shap...  40.4 us
    unnamed x86, local copies, waits for them, and re-layouts  19 us
    dot_general x1, matrix products, per_device(): lax.dot_general(own, w1, (((1,), (1,)), ((0,), (0,))), preferred_element_...  10.3 us
  transfers between devices with their start and end apart: 4, of which 1 were waited for; matrix products, arithmetic and copies ran while one was open for 9% of the time, Pallas kernels for 76%

commit v1 on v0

--- a/solution.py
+++ b/solution.py
@@ -175,7 +175,7 @@
             ],
         ),
         input_output_aliases=aliases,
-        compiler_params=pltpu.CompilerParams(vmem_limit_bytes=44 * MIB),
+        compiler_params=pltpu.CompilerParams(vmem_limit_bytes=60 * MIB),
         cost_estimate=pl.CostEstimate(
             flops=groups * 40 * channels * BINS * LANES * 8 * depth,
             bytes_accessed=80 * MIB,
@@ -285,7 +285,7 @@
             big,
         ],
         out_specs=[big] * 3,
-        compiler_params=pltpu.CompilerParams(vmem_limit_bytes=56 * MIB),
+        compiler_params=pltpu.CompilerParams(vmem_limit_bytes=60 * MIB),
         cost_estimate=pl.CostEstimate(
             flops=2 * passes * wide * hidden * boxes,
             bytes_accessed=passes * wide * hidden * 24 + passes * boxes * (wide + hidden) * 2,
@@ -327,7 +327,7 @@
     images, parts, mine,
     part_ref, weight_ref, box_ref, count_ref,
     back_ref, grad_ref,
-    sums, landed, own, counts, turned, cols, kept,
+    sums, landed, own, counts, split, cols, kept,
     rs_send, rs_recv, ag_send, ag_recv, up_send, up_recv, down_send, down_recv, own_sem,
     count_send, count_recv, col_send, col_recv, kept_send, kept_recv,
 ):
@@ -478,17 +478,21 @@
 
     span = grad_ref.shape[1]
 
-    def columns(p, mask):
-        return turned.at[p, :, pl.ds(pl.multiple_of(peer(mask) * span, span), span), :]
-
     def hand(p, mask):
         return pltpu.make_async_remote_copy(
-            src_ref=columns(p, mask),
-            dst_ref=cols.at[p, mask],
+            src_ref=split.at[p, :, peer(mask)],
+            dst_ref=cols.at[p, :, me],
             send_sem=col_send.at[p, mask],
             recv_sem=col_recv.at[p, mask],
             device_id={"narrow": peer(mask)},
         )
+
+    def handed(p, mask):
+        spot = cols.at[p, :, peer(mask)]
+        pltpu.make_async_remote_copy(
+            src_ref=spot, dst_ref=spot, send_sem=col_send.at[p, mask], recv_sem=col_recv.at[p, mask],
+            device_id={"narrow": peer(mask)},
+        ).wait_recv()
 
     for copy in counting:
         copy.wait_recv()
@@ -532,8 +536,9 @@
             kept[p, me, :, at : at + value.shape[1]] = value
             at += value.shape[1]
         advance_kept(p, 0, 0)
-        turned[p, 0] = hid1.T
-        turned[p, 1] = hid2.T
+        for owner in range(parts):
+            split[p, 0, owner] = hid1[:, owner * span : (owner + 1) * span]
+            split[p, 1, owner] = hid2[:, owner * span : (owner + 1) * span]
         for mask in range(1, parts):
             hand(p, mask).start()
     for p in range(2):
@@ -585,17 +590,18 @@
     loss = jnp.zeros((1, 1), jnp.float32)
     for p in range(2):
         arrive_kept(p, 0, bits - 1)
-        two, head = [], []
-        for mask in range(parts):
-            if mask:
-                hand(p, mask).wait_recv()
-            mine_ref = cols.at[p, mask] if mask else columns(p, 0)
-            slopes = kept.at[p, peer(mask)]
-            two.append(jnp.dot(mine_ref[0], slopes[:, :hidden], preferred_element_type=jnp.float32))
-            head.append(jnp.dot(mine_ref[1], slopes[:, hidden:-LANES], preferred_element_type=jnp.float32))
-            loss += jnp.sum(slopes[:, -LANES:].astype(jnp.float32), keepdims=True)
-        grad_ref[p, :, :hidden] = sum(two)
-        grad_ref[p, :, hidden:] = sum(head)
+        for mask in range(1, parts):
+            handed(p, mask)
+        for k in range(2):
+            cols[p, k, me] = split[p, k, me]
+        slopes = kept[p].reshape(parts * mine, kept.shape[3])
+        down = (((0,), (0,)), ((), ()))
+        for k, (start, stop) in enumerate(((0, hidden), (hidden, grad_ref.shape[2]))):
+            left = cols[p, k].reshape(parts * mine, span)
+            grad_ref[p, :, start:stop] = lax.dot_general(
+                left, slopes[:, start:stop], down, preferred_element_type=jnp.float32
+            )
+        loss += jnp.sum(slopes[:, grad_ref.shape[2] :].astype(jnp.float32), keepdims=True)
     corner = grad_ref[0, 0:8, grad_ref.shape[2] - LANES :]
     place = [lax.broadcasted_iota(jnp.int32, corner.shape, k) for k in range(2)]
     corner = jnp.where((place[0] == 0) & (place[1] == LANES - 1), loss, corner)
@@ -654,8 +660,8 @@
             pltpu.VMEM((passes, parts, mine, hidden), jnp.float32),
             pltpu.VMEM((passes, mine, hidden), low),
             pltpu.VMEM((images, 8, LANES), jnp.float32),
-            pltpu.VMEM((passes, 2, hidden, mine), low),
-            pltpu.VMEM((passes, parts, 2, span, mine), low),
+            pltpu.VMEM((passes, 2, parts, mine, span), low),
+            pltpu.VMEM((passes, 2, parts, mine, span), low),
             pltpu.VMEM((passes, parts, mine, hidden + outs + LANES), low),
             dma((passes, parts)),
             dma((passes, parts)),
@@ -685,29 +691,32 @@
     )(part, weight, box, count)
 
 
-def small_kernel(grad_ref, *refs):
-    at = 0
-    for k in range(2):
-        weight, moment, second = (r[...] for r in refs[3 * k : 3 * k + 3])
-        new = adamw(weight, moment, second, grad_ref[:, at : at + weight.shape[1]])
-        for ref, value in zip(refs[6 + 3 * k : 9 + 3 * k], new):
-            ref[...] = value
-        at += weight.shape[1]
-
-
-def update_small(grad, *arrays):
-    def spec(x):
-        return pl.BlockSpec((None,) + x.shape[1:], lambda p: (p, 0, 0))
-
-    return pl.pallas_call(
+def small_kernel(grad_ref, count_ref, *refs):
+    hidden = refs[0].shape[2]
+    outs = refs[3].shape[0]
+    new = adamw(*(r[...] for r in refs[:3]), grad_ref[:, :, :hidden])
+    for ref, value in zip(refs[6:9], new):
+        ref[...] = value
+    for p in range(grad_ref.shape[0]):
+        grad = grad_ref[p, :, hidden:].T[:outs]
+        new = adamw(*(r[:, p, :] for r in refs[3:6]), grad)
+        for ref, value in zip(refs[9:12], new):
+            ref[:, p, :] = value
+    total = grad_ref[0, 0:1, grad_ref.shape[2] - 1 :]
+    lane = lax.broadcasted_iota(jnp.int32, (8, LANES), 1)
+    refs[12][...] = jnp.where(lane == 0, total, count_ref[...])
+
+
+def update_small(grad, count, two, head):
+    arrays = tuple(two) + tuple(x.transpose(2, 0, 1) for x in head)
+    shapes = [jax.ShapeDtypeStruct(x.shape, jnp.float32) for x in arrays]
+    out = pl.pallas_call(
         small_kernel,
-        out_shape=[jax.ShapeDtypeStruct(x.shape, jnp.float32) for x in arrays],
-        grid=(grad.shape[0],),
-        in_specs=[spec(x) for x in (grad,) + arrays],
-        out_specs=[spec(x) for x in arrays],
-        compiler_params=pltpu.CompilerParams(vmem_limit_bytes=24 * MIB),
+        out_shape=shapes + [jax.ShapeDtypeStruct((8, LANES), jnp.float32)],
+        compiler_params=pltpu.CompilerParams(vmem_limit_bytes=30 * MIB),
         name="update_small",
-    )(grad, *arrays)
+    )(grad, jnp.full((8, LANES), count), *arrays)
+    return (out[6][0, :2],), out[:3], tuple(x.transpose(1, 2, 0) for x in out[3:6])
 
 
 def per_device(
@@ -761,9 +770,8 @@
             grad = lax.all_gather(grad, "wide", axis=1, tiled=True)
     new1 = update_first(pooled, back, fc1_w, fc1_m, fc1_v)
     grad, new1 = lax.optimization_barrier((grad, new1))
-    total = grad[0, 0, -1]
-    new = update_small(grad, fc2_w, fc2_m, fc2_v, head_w, head_m, head_v)
-    return (jnp.stack([total, count]),) + tuple(new1) + tuple(new)
+    losses, new2, newh = update_small(grad, count, (fc2_w, fc2_m, fc2_v), (head_w, head_m, head_v))
+    return losses + tuple(new1) + tuple(new2) + tuple(newh)
 
 
 def solution(mesh):

time: 320 us -> 313 us (0.978)
  local copies, waits for them, and re-layouts: 26.5 us -> 15.6 us
  Pallas kernels: 242 us -> 249 us
  waiting for transfers between devices: 5.42 us -> 0.11 us
    unnamed x86 -> x72, local copies, waits for them, and re-layouts: 19 us -> 5.88 us
    all_gather x1, waiting for transfers between devices: 5.32 us -> 0.01 us  [per_device(): lax.all_gather(weight.astype(jnp.bfloat16), 'narrow', axis=1, tiled=True)]
    pallas_call x4, Pallas kernels: 90.1 us -> 95.4 us  [pool(): pl.pallas_call(partial(pool_kernel, channels, side, groups, len(out_shape...]
    pallas_call x1, Pallas kernels: 2.34 us -> 5.66 us  [update_small(): pl.pallas_call(small_kernel, out_shape=shapes + [jax.ShapeDtypeStruct((8,...]
  transfers between devices with their start and end apart: 4 -> 4, of which waited for: 1 -> 0; matrix products, arithmetic and copies ran while one was open for 9% -> 11% of each run, Pallas kernels for 76% -> 79%
where the time goes in v1:
time: 313 us; the launch traced here: 308 us
  Pallas kernels  249 us (80%)
  local copies, waits for them, and re-layouts  15.6 us (5%)
  between operations  15.4 us (5%)
  other arithmetic  15.1 us (5%)
  matrix products  12.2 us (4%)
    pallas_call x1, Pallas kernels, head_step(): pl.pallas_call(partial(head_kernel, images, parts, mine), out_shape=[jax....  107 us
    pallas_call x4, Pallas kernels, pool(): pl.pallas_call(partial(pool_kernel, channels, side, groups, len(out_shape...  95.4 us
    pallas_call x1, Pallas kernels, update_first(): pl.pallas_call(update_kernel, out_shape=[jax.ShapeDtypeStruct(weight.shap...  40.6 us
    dot_general x1, matrix products, per_device(): lax.dot_general(own, w1, (((1,), (1,)), ((0,), (0,))), preferred_element_...  11.8 us
  transfers between devices with their start and end apart: 4, of which 0 were waited for; matrix products, arithmetic and copies ran while one was open for 11% of the time, Pallas kernels for 79%

profile of v1, /device:TPU:0, one launch (start us, length us, event | category | flops | bytes accessed | tf_op | source)
XLA Modules:
  0.0 308.2 jit_solution(15709711770206748985)
XLA Ops:
  7.2 1.3 convert.24
  8.5 1.2 convert.25
  9.7 0.2 copy.178
  9.9 0.9 fusion.10
  11.0 0.4 convert_reduce_fusion
  11.5 0.5 fusion.8
  12.0 0.1 minimum_reduce_fusion.7
  12.3 0.1 reduce_min.187
  12.4 0.1 reduce_min.190
  12.6 0.1 reduce_min.196
  12.8 0.1 reduce_min.202
  13.0 0.1 reduce_min.205
  13.2 0.1 reduce_min.211
  13.4 0.1 reduce_min.217
  13.6 0.1 reduce_max.203
  13.7 0.1 reduce_max.209
  13.9 0.1 reduce_max.212
  14.1 0.1 reduce_max.218
  14.3 0.1 reduce_max.224
  14.5 0.1 reduce_max.227
  14.7 0.1 reduce_max.233
  15.5 0.6 reshape.1645.span_ref
  16.7 0.7 reshape.1646.table_ref
  17.4 0.2 copy.225
  17.6 0.1 copy.226
  17.7 0.1 select_maximum_fusion
  17.9 0.4 copy.176
  18.3 0.3 copy-done.15
  18.5 0.6 fusion.45
  19.2 0.6 pad_add_fusion.pick_ref
  19.8 0.3 reduce-precision_convert_fusion
  20.1 1.5 pad_maximum_fusion.1.feat_ref
  21.6 0.3 reduce-precision_convert_fusion.1
  21.9 1.5 pad_maximum_fusion
  23.4 24.4 %pool_rois.4 = (bf16[2,1568,2048]{2,1,0:T(8,128)(2,1)}, bf16[2,1568,512]{2,1,0:T(8,128)(2,1)}) custom-call(s32[2]{0:T(128)} %pad_add_fusion.pick_ref, s32[136]{0:T(256)} %reshape.1645.span_ref, bf16[1,3840,128]{2,1,0:T(8,128)(2,1)} %pad_maximum_fusion.1.feat_ref, f32[1,8,8,128]{3,2,1,0:T(8,128)} %reshape.1646.table_ref), custom_call_target="tpu_custom_call" | custom-call | flops 9395240960 | bytes 83886080 | tf_op jit(solution)/shard_map/pool_rois/pallas_call | solution.py:159
  47.8 11.8 %fusion.part_ref = f32[2,512,1024]{2,1,0:T(8,128)} fusion(bf16[2,1568,512]{2,1,0:T(8,128)(2,1)} %get-tuple-element.33, f32[2,1568,1024]{2,1,0:T(8,128)} %w_ref.1), kind=kOutput, calls=%fused_computation | convolution fusion | flops 3291545600 | bytes 20250624 | tf_op jit(solution)/shard_map/dot_general | solution.py:749
  59.6 0.3 reduce-scatter.2.cloned.1.call-start
  60.0 0.3 fusion.16
  60.4 0.1 copy.191
  61.2 0.6 pad_add_fusion.2.pick_ref
  61.8 0.6 pad_add_fusion.1.pick_ref
  62.4 2.2 copy-done
  64.5 107.2 %head_step.1 = (bf16[2,2048,1024]{2,1,0:T(8,128)(2,1)}, f32[2,128,1536]{2,1,0:T(8,128)}) custom-call(f32[2,512,1024]{2,1,0:T(8,128)S(1)} %copy-done, bf16[2,1024,1536]{2,1,0:T(8,128)(2,1)} %all-gather.5.cloned.1.call-done.weight_ref, f32[2,64,128]{2,1,0:T(8,128)S(1)} %pad.25.box_ref, f32[8,128]{1,0:T(8,128)S(1)} %broadcast_in_dim.127.count_ref), custom_call_target="tpu_custom_call" | custom-call | flops 1610612736 | bytes 104857600 | tf_op jit(solution)/shard_map/head_step/pallas_call | solution.py:650
  171.7 0.5 all-gather.7.cloned.1.call-start
  172.3 0.8 slice.89
  173.2 0.2 minimum_reduce_fusion
  176.0 0.1 copy.199
  176.8 0.8 reshape.1649.table_ref
  177.7 0.1 copy.197
  177.8 0.1 copy.198
  177.9 0.1 copy.195
  178.0 0.1 copy.196
  178.2 0.7 reshape.1648.span_ref
  178.9 24.0 %pool_rois.5.refs_0_ = bf16[2,1568,2048]{2,1,0:T(8,128)(2,1)} custom-call(s32[2]{0:T(128)} %pad_add_fusion.2.pick_ref, s32[544]{0:T(1024)} %reshape.1648.span_ref, bf16[4,3888,128]{2,1,0:T(8,128)(2,1)} %bitcast.232, f32[4,8,8,128]{3,2,1,0:T(8,128)} %reshape.1649.table_ref, ...), custom_call_target="tpu_custom_call", output_to_operand_aliasing={{}: (4, {})} | custom-call | flops 9395240960 | bytes 83886080 | tf_op jit(solution)/shard_map/pool_rois/pallas_call | solution.py:159
  202.9 23.6 %pool_rois.6.refs_0_ = bf16[2,1568,2048]{2,1,0:T(8,128)(2,1)} custom-call(s32[2]{0:T(128)} %pad_add_fusion.1.pick_ref, s32[544]{0:T(1024)} %reshape.1648.span_ref, bf16[4,3888,128]{2,1,0:T(8,128)(2,1)} %bitcast.233, f32[4,8,8,128]{3,2,1,0:T(8,128)} %reshape.1649.table_ref, bf16[2,1568,2048]{2,1,0:T(8,128)(2,1)} %pool_rois.5.refs_0_), custom_call_target="tpu_custom_call", output_to_operand_aliasing={{}: (4, {})} | custom-call | flops 9395240960 | bytes 83886080 | tf_op jit(solution)/shard_map/pool_rois/pallas_call | solution.py:159
  226.5 0.6 pad_add_fusion.3.pick_ref
  227.1 0.6 convert_reduce_fusion.1
  227.7 23.5 %pool_rois.7.pooled_ref = bf16[2,1568,2048]{2,1,0:T(8,128)(2,1)} custom-call(s32[2]{0:T(128)} %pad_add_fusion.3.pick_ref, s32[544]{0:T(1024)} %reshape.1648.span_ref, bf16[4,3888,128]{2,1,0:T(8,128)(2,1)} %bitcast.234, f32[4,8,8,128]{3,2,1,0:T(8,128)} %reshape.1649.table_ref, bf16[2,1568,2048]{2,1,0:T(8,128)(2,1)} %pool_rois.6.refs_0_), custom_call_target="tpu_custom_call", output_to_operand_aliasing={{}: (4, {})} | custom-call | flops 9395240960 | bytes 83886080 | tf_op jit(solution)/shard_map/pool_rois/pallas_call | solution.py:159
  251.2 40.6 %update_first.1 = (f32[2,1568,1024]{2,1,0:T(8,128)}, f32[2,1568,1024]{2,1,0:T(8,128)}, f32[2,1568,1024]{2,1,0:T(8,128)}) custom-call(bf16[2,1568,2048]{2,1,0:T(8,128)(2,1)} %pool_rois.7.pooled_ref, bf16[2,2048,1024]{2,1,0:T(8,128)(2,1)} %get-tuple-element.41.back_ref, f32[2,1568,1024]{2,1,0:T(8,128)} %w_ref.1, f32[2,1568,1024]{2,1,0:T(8,128)} %m_ref.1, ...), custom_call_target="tpu_custom_call" | custom-call | flops 13153337344 | bytes 98304000 | tf_op jit(solution)/shard_map/update_first/pallas_call | solution.py:276
  291.9 0.6 broadcast_in_dim.133.count_ref
  292.6 1.4 copy-done.3
  294.0 1.2 copy-done.5
  295.2 5.7 %update_small.1 = (f32[2,128,1024]{2,1,0:T(8,128)}, f32[2,128,1024]{2,1,0:T(8,128)}, f32[2,128,1024]{2,1,0:T(8,128)}, f32[401,2,128]{2,1,0:T(2,128)}, f32[401,2,...) custom-call(f32[2,128,1536]{2,1,0:T(8,128)S(1)} %copy-done.3, ...), custom_call_target="tpu_custom_call" | custom-call | tf_op jit(solution)/shard_map/update_small/pallas_call | solution.py:713
  300.9 0.5 slice_bitcast_fusion.2
  (174 shorter events, 6.1 us)
Async XLA Ops:
  7.2 52.4 %all-gather.5.cloned.1.call-start = ((), (), s32[]{:S(2)}) async-start(), calls=%async_computation.1 | async-start | bytes 7077888 | tf_op jit(solution)/shard_map/all_gather | solution.py:744
  8.5 2.4 copy-start.11
  8.5 2.4 copy-start.14
  9.9 7.5 %copy-start.10 = (f32[1,32,16,16]{1,3,2,0:T(8,128)S(1)}, f32[1,32,16,16]{1,3,2,0:T(8,128)}, u32[]{:S(2)}) copy-start(f32[1,32,16,16]{1,3,2,0:T(8,128)} %param.20) | copy-start | bytes 98308
  9.9 7.7 %copy-start.12 = (f32[1,32,8,8]{1,3,2,0:T(8,128)S(1)}, f32[1,32,8,8]{1,3,2,0:T(8,128)}, u32[]{:S(2)}) copy-start(f32[1,32,8,8]{1,3,2,0:T(8,128)} %param.21) | copy-start | bytes 24580
  9.9 7.8 %copy-start.8 = (f32[1,32,64,64]{3,2,1,0:T(8,128)S(1)}, f32[1,32,64,64]{3,2,1,0:T(8,128)}, u32[]{:S(2)}) copy-start(f32[1,32,64,64]{3,2,1,0:T(8,128)} %param.18) | copy-start | bytes 1572868
  9.9 7.8 %copy-start.9 = (f32[1,32,32,32]{3,2,1,0:T(8,128)S(1)}, f32[1,32,32,32]{3,2,1,0:T(8,128)}, u32[]{:S(2)}) copy-start(f32[1,32,32,32]{3,2,1,0:T(8,128)} %param.19) | copy-start | bytes 393220
  10.9 161.4 %all-gather.9.cloned.1.call-start = ((), (), s32[]{:S(2)}) async-start(), calls=%async_computation.4 | async-start | bytes 4976640 | tf_op jit(solution)/shard_map/all_gather | solution.py:751
  17.9 0.7 copy-start.15
  47.8 12.1 %copy-start.16 = (s32[2,1,512]{2,1,0:T(1,128)S(1)}, s32[2,1,512]{2,1,0:T(1,128)}, u32[]{:S(2)}) copy-start(s32[2,1,512]{2,1,0:T(1,128)} %param.24) | copy-start | bytes 12292
  47.8 12.1 %copy-start.13 = (f32[2,1,512,4]{2,3,1,0:T(4,128)S(1)}, f32[2,1,512,4]{2,3,1,0:T(4,128)}, u32[]{:S(2)}) copy-start(f32[2,1,512,4]{2,3,1,0:T(4,128)} %param.26) | copy-start | bytes 49156
  59.6 166.8 %reduce-scatter.2.cloned.1.call-start = ((), (), s32[]{:S(2)}) async-start(), calls=%async_computation.2 | async-start | bytes 1966080 | tf_op jit(solution)/shard_map/reduce_scatter | solution.py:760
  62.4 2.2 copy-start
  171.7 120.1 %all-gather.7.cloned.1.call-start = ((), (), s32[]{:S(2)}) async-start(), calls=%async_computation.3 | async-start | bytes 1966080 | tf_op jit(solution)/shard_map/all_gather | solution.py:770
  251.2 41.4 %copy-start.1 = (f32[2,128,1024]{2,1,0:T(8,128)S(1)}, f32[2,128,1024]{2,1,0:T(8,128)}, u32[]{:S(2)}) copy-start(f32[2,128,1024]{2,1,0:T(8,128)} %refs_0_.1) | copy-start | bytes 3145732
  251.2 41.4 %copy-start.2 = (f32[2,128,401]{1,0,2:T(2,128)S(1)}, f32[2,128,401]{1,0,2:T(2,128)}, u32[]{:S(2)}) copy-start(f32[2,128,401]{1,0,2:T(2,128)} %param.33) | copy-start | bytes 1231876
  251.2 41.4 %copy-start.4 = (f32[2,128,1024]{2,1,0:T(8,128)S(1)}, f32[2,128,1024]{2,1,0:T(8,128)}, u32[]{:S(2)}) copy-start(f32[2,128,1024]{2,1,0:T(8,128)} %refs_1_.1) | copy-start | bytes 3145732
  251.2 41.4 %copy-start.6 = (f32[2,128,401]{1,0,2:T(2,128)S(1)}, f32[2,128,401]{1,0,2:T(2,128)}, u32[]{:S(2)}) copy-start(f32[2,128,401]{1,0,2:T(2,128)} %param.34) | copy-start | bytes 1231876
  251.2 41.4 %copy-start.7 = (f32[2,128,401]{1,0,2:T(2,128)S(1)}, f32[2,128,401]{1,0,2:T(2,128)}, u32[]{:S(2)}) copy-start(f32[2,128,401]{1,0,2:T(2,128)} %param.35) | copy-start | bytes 1231876
  292.6 1.4 copy-start.3
  294.0 1.2 copy-start.5
Sparse Core Ops, SparseCore 0:
  11.0 48.2 all-gather.4
  61.5 91.6 all-gather.8
  171.9 33.5 reduce-scatter.1
  226.6 35.8 all-gather.6

commit v2 on v1

--- a/solution.py
+++ b/solution.py
@@ -361,46 +361,48 @@
             )
         )
 
-    def scatter(p, mask, bit, source):
+    part = mine // 2
+
+    def scatter(q, mask, bit, source):
         return pltpu.make_async_remote_copy(
             src_ref=source,
-            dst_ref=landed.at[p, mask],
-            send_sem=rs_send.at[p, mask],
-            recv_sem=rs_recv.at[p, mask],
+            dst_ref=landed.at[q, mask],
+            send_sem=rs_send.at[q, mask],
+            recv_sem=rs_recv.at[q, mask],
             device_id={"narrow": peer(1 << bit)},
         )
 
-    def part_at(p, mask):
-        return part_ref.at[p, pl.ds(pl.multiple_of(peer(mask) * mine, mine), mine), :]
+    def part_at(q, mask):
+        start = peer(mask) * mine + q % 2 * part
+        return part_ref.at[q // 2, pl.ds(pl.multiple_of(start, part), part), :]
 
     copies = {}
-    for p in range(2):
+    for q in range(4):
         for mask in range(1, parts, 2):
-            copies[p, mask] = scatter(p, mask, 0, part_at(p, mask))
-            copies[p, mask].start()
+            copies[q, mask] = scatter(q, mask, 0, part_at(q, mask))
+            copies[q, mask].start()
 
     def stage(p, at):
-        order = [0] + orders[p]
-        bit = order[at - 1]
-        seen = sum(1 << b for b in order[:at])
-        for mask in range(parts):
-            if mask & seen:
-                continue
-            copies[p, mask | 1 << bit].wait_recv()
-            if at == 1:
-                have = part_ref[p, pl.ds(pl.multiple_of(peer(mask) * mine, mine), mine), :]
-            else:
-                have = sums[p, mask]
-            sums[p, mask] = have + landed[p, mask | 1 << bit]
-            if at < bits and mask >> order[at] & 1:
-                copies[p, mask] = scatter(p, mask, order[at], sums.at[p, mask])
-                copies[p, mask].start()
+        for q in (2 * p, 2 * p + 1):
+            order = [0] + orders[q % 2]
+            bit = order[at - 1]
+            seen = sum(1 << b for b in order[:at])
+            masks = [m for m in range(parts) if not m & seen]
+            if at < bits:
+                masks.sort(key=lambda m: not m >> order[at] & 1)
+            for mask in masks:
+                copies[q, mask | 1 << bit].wait_recv()
+                have = part_at(q, mask)[...] if at == 1 else sums[q, mask]
+                sums[q, mask] = have + landed[q, mask | 1 << bit]
+                if at < bits and mask >> order[at] & 1:
+                    copies[q, mask] = scatter(q, mask, order[at], sums.at[q, mask])
+                    copies[q, mask].start()
 
     for copy in counting:
         copy.start()
     for at in range(1, bits):
-        for p in range(2):
-            stage(p, at)
+        stage(0, at)
+    stage(1, 1)
 
     def rows(p, image, mask):
         place = (image * parts + peer(mask)) * mine
@@ -499,8 +501,9 @@
     count = count_ref[0:1, 0:1] + sum(counts[k, 0:1, 0:1] for k in range(1, images))
     hidden = part_ref.shape[2]
     for p in range(2):
-        stage(p, bits)
-        pre1 = sums[p, 0]
+        for at in range(2 if p else bits, bits + 1):
+            stage(p, at)
+        pre1 = jnp.concatenate([sums[2 * p, 0], sums[2 * p + 1, 0]], axis=0)
         sig1 = sigmoid(pre1)
         hid1 = (pre1 * sig1).astype(jnp.bfloat16)
         pre2 = jnp.dot(hid1, weight_ref[p, :, :hidden], preferred_element_type=jnp.float32)
@@ -632,9 +635,9 @@
                     hop(p, d, up).wait_send()
 
         each_side(d, do)
-    for p in range(2):
+    for q in range(4):
         for mask in range(1, parts):
-            copies[p, mask].wait_send()
+            copies[q, mask].wait_send()
     for copy in counting:
         copy.wait_send()
 
@@ -656,15 +659,15 @@
         in_specs=[vmem] * 4,
         out_specs=[pl.BlockSpec(memory_space=pl.ANY), vmem],
         scratch_shapes=[
-            pltpu.VMEM((passes, parts, mine, hidden), jnp.float32),
-            pltpu.VMEM((passes, parts, mine, hidden), jnp.float32),
+            pltpu.VMEM((2 * passes, parts, mine // 2, hidden), jnp.float32),
+            pltpu.VMEM((2 * passes, parts, mine // 2, hidden), jnp.float32),
             pltpu.VMEM((passes, mine, hidden), low),
             pltpu.VMEM((images, 8, LANES), jnp.float32),
             pltpu.VMEM((passes, 2, parts, mine, span), low),
             pltpu.VMEM((passes, 2, parts, mine, span), low),
             pltpu.VMEM((passes, parts, mine, hidden + outs + LANES), low),
-            dma((passes, parts)),
-            dma((passes, parts)),
+            dma((2 * passes, parts)),
+            dma((2 * passes, parts)),
             dma((passes, images, parts)),
             dma((passes, images, parts)),
             dma((passes, images)),

time: 313 us -> 314 us (level)
  transfers between devices with their start and end apart: 4 -> 4, of which waited for: 0 -> 1; matrix products, arithmetic and copies ran while one was open for 11% -> 11% of each run, Pallas kernels for 79% -> 79%
where the time goes in v2:
time: 314 us; the launch traced here: 309 us
  Pallas kernels  249 us (79%)
  local copies, waits for them, and re-layouts  15.6 us (5%)
  between operations  15.4 us (5%)
  other arithmetic  15.1 us (5%)
  matrix products  12.3 us (4%)
    pallas_call x1, Pallas kernels, head_step(): pl.pallas_call(partial(head_kernel, images, parts, mine), out_shape=[jax....  108 us
    pallas_call x4, Pallas kernels, pool(): pl.pallas_call(partial(pool_kernel, channels, side, groups, len(out_shape...  94.7 us
    pallas_call x1, Pallas kernels, update_first(): pl.pallas_call(update_kernel, out_shape=[jax.ShapeDtypeStruct(weight.shap...  40.7 us
    dot_general x1, matrix products, per_device(): lax.dot_general(own, w1, (((1,), (1,)), ((0,), (0,))), preferred_element_...  11.8 us
  transfers between devices with their start and end apart: 4, of which 1 were waited for; matrix products, arithmetic and copies ran while one was open for 11% of the time, Pallas kernels for 79%

profile of v2, /device:TPU:0, one launch (start us, length us, event | category | flops | bytes accessed | tf_op | source)
XLA Modules:
  0.0 308.7 jit_solution(17825174378925852835)
XLA Ops:
  7.2 1.3 convert.24
  8.5 1.2 convert.25
  9.7 0.2 copy.178
  9.9 0.9 fusion.10
  11.0 0.4 convert_reduce_fusion
  11.5 0.5 fusion.8
  12.0 0.1 minimum_reduce_fusion.7
  12.3 0.1 reduce_min.187
  12.4 0.1 reduce_min.190
  12.6 0.1 reduce_min.196
  12.8 0.1 reduce_min.202
  13.0 0.1 reduce_min.205
  13.2 0.1 reduce_min.211
  13.4 0.1 reduce_min.217
  13.6 0.1 reduce_max.203
  13.7 0.1 reduce_max.209
  13.9 0.1 reduce_max.212
  14.1 0.1 reduce_max.218
  14.3 0.1 reduce_max.224
  14.5 0.1 reduce_max.227
  14.7 0.1 reduce_max.233
  15.5 0.6 reshape.1645.span_ref
  16.7 0.7 reshape.1646.table_ref
  17.4 0.2 copy.225
  17.6 0.1 copy.226
  17.7 0.1 select_maximum_fusion
  17.9 0.4 copy.176
  18.3 0.3 copy-done.15
  18.5 0.6 fusion.45
  19.2 0.6 pad_add_fusion.pick_ref
  19.8 0.3 reduce-precision_convert_fusion
  20.1 1.5 pad_maximum_fusion.1.feat_ref
  21.6 0.3 reduce-precision_convert_fusion.1
  21.9 1.5 pad_maximum_fusion
  23.4 23.9 %pool_rois.4 = (bf16[2,1568,2048]{2,1,0:T(8,128)(2,1)}, bf16[2,1568,512]{2,1,0:T(8,128)(2,1)}) custom-call(s32[2]{0:T(128)} %pad_add_fusion.pick_ref, s32[136]{0:T(256)} %reshape.1645.span_ref, bf16[1,3840,128]{2,1,0:T(8,128)(2,1)} %pad_maximum_fusion.1.feat_ref, f32[1,8,8,128]{3,2,1,0:T(8,128)} %reshape.1646.table_ref), custom_call_target="tpu_custom_call" | custom-call | flops 9395240960 | bytes 83886080 | tf_op jit(solution)/shard_map/pool_rois/pallas_call | solution.py:159
  47.3 11.8 %fusion.part_ref = f32[2,512,1024]{2,1,0:T(8,128)} fusion(bf16[2,1568,512]{2,1,0:T(8,128)(2,1)} %get-tuple-element.33, f32[2,1568,1024]{2,1,0:T(8,128)} %w_ref.1), kind=kOutput, calls=%fused_computation | convolution fusion | flops 3291545600 | bytes 20250624 | tf_op jit(solution)/shard_map/dot_general | solution.py:752
  59.1 0.2 all-gather.5.cloned.1.call-done.weight_ref
  59.4 0.3 reduce-scatter.2.cloned.1.call-start
  59.8 0.3 fusion.16
  60.2 0.1 copy.191
  61.0 0.6 pad_add_fusion.2.pick_ref
  61.5 0.6 pad_add_fusion.1.pick_ref
  62.1 2.2 copy-done
  64.3 108.0 %head_step.1 = (bf16[2,2048,1024]{2,1,0:T(8,128)(2,1)}, f32[2,128,1536]{2,1,0:T(8,128)}) custom-call(f32[2,512,1024]{2,1,0:T(8,128)S(1)} %copy-done, bf16[2,1024,1536]{2,1,0:T(8,128)(2,1)} %all-gather.5.cloned.1.call-done.weight_ref, f32[2,64,128]{2,1,0:T(8,128)S(1)} %pad.25.box_ref, f32[8,128]{1,0:T(8,128)S(1)} %broadcast_in_dim.127.count_ref), custom_call_target="tpu_custom_call" | custom-call | flops 1610612736 | bytes 104857600 | tf_op jit(solution)/shard_map/head_step/pallas_call | solution.py:653
  172.4 0.5 all-gather.7.cloned.1.call-start
  172.9 0.8 slice.89
  173.8 0.2 minimum_reduce_fusion
  176.7 0.1 copy.199
  177.5 0.8 reshape.1649.table_ref
  178.4 0.1 copy.198
  178.6 0.1 copy.195
  178.7 0.1 copy.196
  178.8 0.7 reshape.1648.span_ref
  179.5 23.5 %pool_rois.5.refs_0_ = bf16[2,1568,2048]{2,1,0:T(8,128)(2,1)} custom-call(s32[2]{0:T(128)} %pad_add_fusion.2.pick_ref, s32[544]{0:T(1024)} %reshape.1648.span_ref, bf16[4,3888,128]{2,1,0:T(8,128)(2,1)} %bitcast.232, f32[4,8,8,128]{3,2,1,0:T(8,128)} %reshape.1649.table_ref, ...), custom_call_target="tpu_custom_call", output_to_operand_aliasing={{}: (4, {})} | custom-call | flops 9395240960 | bytes 83886080 | tf_op jit(solution)/shard_map/pool_rois/pallas_call | solution.py:159
  203.0 23.5 %pool_rois.6.refs_0_ = bf16[2,1568,2048]{2,1,0:T(8,128)(2,1)} custom-call(s32[2]{0:T(128)} %pad_add_fusion.1.pick_ref, s32[544]{0:T(1024)} %reshape.1648.span_ref, bf16[4,3888,128]{2,1,0:T(8,128)(2,1)} %bitcast.233, f32[4,8,8,128]{3,2,1,0:T(8,128)} %reshape.1649.table_ref, bf16[2,1568,2048]{2,1,0:T(8,128)(2,1)} %pool_rois.5.refs_0_), custom_call_target="tpu_custom_call", output_to_operand_aliasing={{}: (4, {})} | custom-call | flops 9395240960 | bytes 83886080 | tf_op jit(solution)/shard_map/pool_rois/pallas_call | solution.py:159
  226.6 0.6 pad_add_fusion.3.pick_ref
  227.2 0.6 convert_reduce_fusion.1
  227.8 23.8 %pool_rois.7.pooled_ref = bf16[2,1568,2048]{2,1,0:T(8,128)(2,1)} custom-call(s32[2]{0:T(128)} %pad_add_fusion.3.pick_ref, s32[544]{0:T(1024)} %reshape.1648.span_ref, bf16[4,3888,128]{2,1,0:T(8,128)(2,1)} %bitcast.234, f32[4,8,8,128]{3,2,1,0:T(8,128)} %reshape.1649.table_ref, bf16[2,1568,2048]{2,1,0:T(8,128)(2,1)} %pool_rois.6.refs_0_), custom_call_target="tpu_custom_call", output_to_operand_aliasing={{}: (4, {})} | custom-call | flops 9395240960 | bytes 83886080 | tf_op jit(solution)/shard_map/pool_rois/pallas_call | solution.py:159
  251.6 40.7 %update_first.1 = (f32[2,1568,1024]{2,1,0:T(8,128)}, f32[2,1568,1024]{2,1,0:T(8,128)}, f32[2,1568,1024]{2,1,0:T(8,128)}) custom-call(bf16[2,1568,2048]{2,1,0:T(8,128)(2,1)} %pool_rois.7.pooled_ref, bf16[2,2048,1024]{2,1,0:T(8,128)(2,1)} %get-tuple-element.41.back_ref, f32[2,1568,1024]{2,1,0:T(8,128)} %w_ref.1, f32[2,1568,1024]{2,1,0:T(8,128)} %m_ref.1, ...), custom_call_target="tpu_custom_call" | custom-call | flops 13153337344 | bytes 98304000 | tf_op jit(solution)/shard_map/update_first/pallas_call | solution.py:276
  292.3 0.6 broadcast_in_dim.133.count_ref
  293.1 1.4 copy-done.3
  294.5 1.2 copy-done.5
  295.7 5.7 %update_small.1 = (f32[2,128,1024]{2,1,0:T(8,128)}, f32[2,128,1024]{2,1,0:T(8,128)}, f32[2,128,1024]{2,1,0:T(8,128)}, f32[401,2,128]{2,1,0:T(2,128)}, f32[401,2,...) custom-call(f32[2,128,1536]{2,1,0:T(8,128)S(1)} %copy-done.3, ...), custom_call_target="tpu_custom_call" | custom-call | tf_op jit(solution)/shard_map/update_small/pallas_call | solution.py:716
  301.3 0.5 slice_bitcast_fusion.2
  (174 shorter events, 6.2 us)
Async XLA Ops:
  7.2 52.2 %all-gather.5.cloned.1.call-start = ((), (), s32[]{:S(2)}) async-start(), calls=%async_computation.1 | async-start | bytes 7077888 | tf_op jit(solution)/shard_map/all_gather | solution.py:747
  8.5 2.4 copy-start.11
  8.5 2.4 copy-start.14
  9.9 7.5 %copy-start.10 = (f32[1,32,16,16]{1,3,2,0:T(8,128)S(1)}, f32[1,32,16,16]{1,3,2,0:T(8,128)}, u32[]{:S(2)}) copy-start(f32[1,32,16,16]{1,3,2,0:T(8,128)} %param.20) | copy-start | bytes 98308
  9.9 7.7 %copy-start.12 = (f32[1,32,8,8]{1,3,2,0:T(8,128)S(1)}, f32[1,32,8,8]{1,3,2,0:T(8,128)}, u32[]{:S(2)}) copy-start(f32[1,32,8,8]{1,3,2,0:T(8,128)} %param.21) | copy-start | bytes 24580
  9.9 7.8 %copy-start.8 = (f32[1,32,64,64]{3,2,1,0:T(8,128)S(1)}, f32[1,32,64,64]{3,2,1,0:T(8,128)}, u32[]{:S(2)}) copy-start(f32[1,32,64,64]{3,2,1,0:T(8,128)} %param.18) | copy-start | bytes 1572868
  9.9 7.8 %copy-start.9 = (f32[1,32,32,32]{3,2,1,0:T(8,128)S(1)}, f32[1,32,32,32]{3,2,1,0:T(8,128)}, u32[]{:S(2)}) copy-start(f32[1,32,32,32]{3,2,1,0:T(8,128)} %param.19) | copy-start | bytes 393220
  10.9 162.0 %all-gather.9.cloned.1.call-start = ((), (), s32[]{:S(2)}) async-start(), calls=%async_computation.4 | async-start | bytes 4976640 | tf_op jit(solution)/shard_map/all_gather | solution.py:754
  17.9 0.7 copy-start.15
  47.3 12.4 %copy-start.16 = (s32[2,1,512]{2,1,0:T(1,128)S(1)}, s32[2,1,512]{2,1,0:T(1,128)}, u32[]{:S(2)}) copy-start(s32[2,1,512]{2,1,0:T(1,128)} %param.24) | copy-start | bytes 12292
  47.3 12.4 %copy-start.13 = (f32[2,1,512,4]{2,3,1,0:T(4,128)S(1)}, f32[2,1,512,4]{2,3,1,0:T(4,128)}, u32[]{:S(2)}) copy-start(f32[2,1,512,4]{2,3,1,0:T(4,128)} %param.26) | copy-start | bytes 49156
  59.4 167.2 %reduce-scatter.2.cloned.1.call-start = ((), (), s32[]{:S(2)}) async-start(), calls=%async_computation.2 | async-start | bytes 1966080 | tf_op jit(solution)/shard_map/reduce_scatter | solution.py:763
  62.1 2.2 copy-start
  172.4 119.9 %all-gather.7.cloned.1.call-start = ((), (), s32[]{:S(2)}) async-start(), calls=%async_computation.3 | async-start | bytes 1966080 | tf_op jit(solution)/shard_map/all_gather | solution.py:773
  251.6 41.4 %copy-start.1 = (f32[2,128,1024]{2,1,0:T(8,128)S(1)}, f32[2,128,1024]{2,1,0:T(8,128)}, u32[]{:S(2)}) copy-start(f32[2,128,1024]{2,1,0:T(8,128)} %refs_0_.1) | copy-start | bytes 3145732
  251.6 41.4 %copy-start.2 = (f32[2,128,401]{1,0,2:T(2,128)S(1)}, f32[2,128,401]{1,0,2:T(2,128)}, u32[]{:S(2)}) copy-start(f32[2,128,401]{1,0,2:T(2,128)} %param.33) | copy-start | bytes 1231876
  251.6 41.4 %copy-start.4 = (f32[2,128,1024]{2,1,0:T(8,128)S(1)}, f32[2,128,1024]{2,1,0:T(8,128)}, u32[]{:S(2)}) copy-start(f32[2,128,1024]{2,1,0:T(8,128)} %refs_1_.1) | copy-start | bytes 3145732
  251.6 41.4 %copy-start.6 = (f32[2,128,401]{1,0,2:T(2,128)S(1)}, f32[2,128,401]{1,0,2:T(2,128)}, u32[]{:S(2)}) copy-start(f32[2,128,401]{1,0,2:T(2,128)} %param.34) | copy-start | bytes 1231876
  251.6 41.5 %copy-start.7 = (f32[2,128,401]{1,0,2:T(2,128)S(1)}, f32[2,128,401]{1,0,2:T(2,128)}, u32[]{:S(2)}) copy-start(f32[2,128,401]{1,0,2:T(2,128)} %param.35) | copy-start | bytes 1231876
  293.1 1.4 copy-start.3
  294.5 1.2 copy-start.5
Sparse Core Ops, SparseCore 0:
  11.0 48.2 all-gather.4
  61.5 89.1 all-gather.8
  172.5 34.1 reduce-scatter.1
  226.7 35.9 all-gather.6

commit v3 on v1

--- a/solution.py
+++ b/solution.py
@@ -16,8 +16,8 @@
 EPSILON = 1e-08
 BINS = 7
 CHUNK = 8
-STATIC = 5
-WINDOW = 24
+STATIC = 4
+WINDOW = 20
 MORE = 4
 SPANS = 17
 LANES = 128
@@ -88,12 +88,12 @@
     def spot(i, j):
         return pl.ds(i * BINS + j, channels, stride=BINS * BINS)
 
-    def work(group, slot, following):
+    def work(group, slot, following, beside):
         for i in range(BINS):
             accs = block(slot, i, span_ref[at(group) + 3 + i], WINDOW)
             for j in range(BINS):
                 line_ref[slot, spot(i, j), :] = accs[j]
-            if i < STATIC:
+            if beside and i < STATIC:
                 fill(following, 1 - slot, span_ref[at(following)] + i * CHUNK)
 
         @pl.when(span_ref[at(group) + 2] > 0)
@@ -118,12 +118,19 @@
 
     group = 2 * step
     weights(group + 1, 1)
-    work(group, 0, group + 1)
+    work(group, 0, group + 1, True)
     rest(group + 1, 1)
-    following = jnp.minimum(group + 2, groups - 1)
-    weights(following, 0)
-    work(group + 1, 1, following)
-    rest(following, 0)
+
+    @pl.when(group + 2 < groups)
+    def _():
+        weights(group + 2, 0)
+        work(group + 1, 1, group + 2, True)
+        rest(group + 2, 0)
+
+    @pl.when(group + 2 >= groups)
+    def _():
+        work(group + 1, 1, group + 1, False)
+
     a, b = line_ref[0], line_ref[1]
     lanes = lax.broadcasted_iota(jnp.int32, a.shape, 1)
     new = [jnp.where(lanes < half, a, pltpu.roll(b, half, 1)), jnp.where(lanes < half, pltpu.roll(a, half, 1), b)]
@@ -535,7 +542,6 @@
         for value in (back_p2, back_z, losses.astype(jnp.bfloat16)):
             kept[p, me, :, at : at + value.shape[1]] = value
             at += value.shape[1]
-        advance_kept(p, 0, 0)
         for owner in range(parts):
             split[p, 0, owner] = hid1[:, owner * span : (owner + 1) * span]
             split[p, 1, owner] = hid2[:, owner * span : (owner + 1) * span]
@@ -570,7 +576,6 @@
         if d == 0:
             for p in range(2):
                 advance(p, level, at)
-                advance_kept(p, 0, at)
         else:
 
             def do(image, up):
@@ -586,6 +591,12 @@
                 enter(d)
             elif 0 < at < bits:
                 go_on(d, at)
+        if tick % 2 and tick // 2 < bits:
+            for p in range(2):
+                advance_kept(p, 0, tick // 2)
+    for at in range((images + bits - 1) // 2, bits):
+        for p in range(2):
+            advance_kept(p, 0, at)
 
     loss = jnp.zeros((1, 1), jnp.float32)
     for p in range(2):

time: 313 us -> 316 us (level)
    pallas_call x1, Pallas kernels: 107 us -> 117 us  [head_step(): pl.pallas_call(partial(head_kernel, images, parts, mine), out_shape=[jax....]
    pallas_call x4, Pallas kernels: 95.4 us -> 85.7 us  [pool(): pl.pallas_call(partial(pool_kernel, channels, side, groups, len(out_shape...]
  transfers between devices with their start and end apart: 4 -> 4, of which waited for: 0 -> 1; matrix products, arithmetic and copies ran while one was open for 11% -> 11% of each run, Pallas kernels for 79% -> 79%
where the time goes in v3:
time: 316 us; the launch traced here: 310 us
  Pallas kernels  249 us (79%)
  local copies, waits for them, and re-layouts  15.6 us (5%)
  between operations  15.2 us (5%)
  other arithmetic  15.1 us (5%)
  matrix products  12.2 us (4%)
    pallas_call x1, Pallas kernels, head_step(): pl.pallas_call(partial(head_kernel, images, parts, mine), out_shape=[jax....  117 us
    pallas_call x4, Pallas kernels, pool(): pl.pallas_call(partial(pool_kernel, channels, side, groups, len(out_shape...  85.7 us
    pallas_call x1, Pallas kernels, update_first(): pl.pallas_call(update_kernel, out_shape=[jax.ShapeDtypeStruct(weight.shap...  41 us
    dot_general x1, matrix products, per_device(): lax.dot_general(own, w1, (((1,), (1,)), ((0,), (0,))), preferred_element_...  11.8 us
  transfers between devices with their start and end apart: 4, of which 1 were waited for; matrix products, arithmetic and copies ran while one was open for 11% of the time, Pallas kernels for 79%

profile of v3, /device:TPU:0, one launch (start us, length us, event | category | flops | bytes accessed | tf_op | source)
XLA Modules:
  0.0 309.8 jit_solution(12063966077136856220)
XLA Ops:
  7.2 1.3 convert.24
  8.5 1.2 convert.25
  9.7 0.2 copy.178
  9.9 0.9 fusion.10
  11.0 0.4 convert_reduce_fusion
  11.5 0.5 fusion.8
  12.0 0.1 minimum_reduce_fusion.7
  12.3 0.1 reduce_min.187
  12.4 0.1 reduce_min.190
  12.6 0.1 reduce_min.196
  12.8 0.1 reduce_min.202
  13.0 0.1 reduce_min.205
  13.2 0.1 reduce_min.211
  13.4 0.1 reduce_min.217
  13.6 0.1 reduce_max.203
  13.7 0.1 reduce_max.209
  13.9 0.1 reduce_max.212
  14.1 0.1 reduce_max.218
  14.3 0.1 reduce_max.224
  14.5 0.1 reduce_max.227
  14.7 0.1 reduce_max.233
  15.5 0.6 reshape.1645.span_ref
  16.7 0.7 reshape.1646.table_ref
  17.4 0.2 copy.225
  17.6 0.1 copy.226
  17.7 0.1 select_maximum_fusion
  17.9 0.4 copy.176
  18.3 0.3 copy-done.15
  18.5 0.6 fusion.45
  19.2 0.6 pad_add_fusion.pick_ref
  19.8 0.3 reduce-precision_convert_fusion
  20.1 1.5 pad_maximum_fusion.1.feat_ref
  21.6 0.3 reduce-precision_convert_fusion.1
  21.9 1.5 pad_maximum_fusion
  23.4 22.5 %pool_rois.4 = (bf16[2,1568,2048]{2,1,0:T(8,128)(2,1)}, bf16[2,1568,512]{2,1,0:T(8,128)(2,1)}) custom-call(s32[2]{0:T(128)} %pad_add_fusion.pick_ref, s32[136]{0:T(256)} %reshape.1645.span_ref, bf16[1,3840,128]{2,1,0:T(8,128)(2,1)} %pad_maximum_fusion.1.feat_ref, f32[1,8,8,128]{3,2,1,0:T(8,128)} %reshape.1646.table_ref), custom_call_target="tpu_custom_call" | custom-call | flops 9395240960 | bytes 83886080 | tf_op jit(solution)/shard_map/pool_rois/pallas_call | solution.py:166
  46.0 11.8 %fusion.part_ref = f32[2,512,1024]{2,1,0:T(8,128)} fusion(bf16[2,1568,512]{2,1,0:T(8,128)(2,1)} %get-tuple-element.33, f32[2,1568,1024]{2,1,0:T(8,128)} %w_ref.1), kind=kOutput, calls=%fused_computation | convolution fusion | flops 3291545600 | bytes 20250624 | tf_op jit(solution)/shard_map/dot_general | solution.py:760
  57.7 1.6 all-gather.5.cloned.1.call-done.weight_ref
  59.4 0.2 reduce-scatter.2.cloned.1.call-start
  59.7 0.3 fusion.16
  60.1 0.1 copy.191
  60.9 0.6 pad_add_fusion.2.pick_ref
  61.5 0.6 pad_add_fusion.1.pick_ref
  62.1 2.2 copy-done
  64.2 117.0 %head_step.1 = (bf16[2,2048,1024]{2,1,0:T(8,128)(2,1)}, f32[2,128,1536]{2,1,0:T(8,128)}) custom-call(f32[2,512,1024]{2,1,0:T(8,128)S(1)} %copy-done, bf16[2,1024,1536]{2,1,0:T(8,128)(2,1)} %all-gather.5.cloned.1.call-done.weight_ref, f32[2,64,128]{2,1,0:T(8,128)S(1)} %pad.25.box_ref, f32[8,128]{1,0:T(8,128)S(1)} %broadcast_in_dim.127.count_ref), custom_call_target="tpu_custom_call" | custom-call | flops 1610612736 | bytes 104857600 | tf_op jit(solution)/shard_map/head_step/pallas_call | solution.py:661
  181.3 0.3 all-gather.7.cloned.1.call-start
  181.6 0.8 slice.89
  182.5 0.2 minimum_reduce_fusion
  185.3 0.1 copy.199
  186.1 0.8 reshape.1649.table_ref
  187.0 0.1 copy.197
  187.1 0.1 copy.198
  187.2 0.1 copy.195
  187.5 0.7 reshape.1648.span_ref
  188.2 21.1 %pool_rois.5.refs_0_ = bf16[2,1568,2048]{2,1,0:T(8,128)(2,1)} custom-call(s32[2]{0:T(128)} %pad_add_fusion.2.pick_ref, s32[544]{0:T(1024)} %reshape.1648.span_ref, bf16[4,3888,128]{2,1,0:T(8,128)(2,1)} %bitcast.232, f32[4,8,8,128]{3,2,1,0:T(8,128)} %reshape.1649.table_ref, ...), custom_call_target="tpu_custom_call", output_to_operand_aliasing={{}: (4, {})} | custom-call | flops 9395240960 | bytes 83886080 | tf_op jit(solution)/shard_map/pool_rois/pallas_call | solution.py:166
  209.2 21.5 %pool_rois.6.refs_0_ = bf16[2,1568,2048]{2,1,0:T(8,128)(2,1)} custom-call(s32[2]{0:T(128)} %pad_add_fusion.1.pick_ref, s32[544]{0:T(1024)} %reshape.1648.span_ref, bf16[4,3888,128]{2,1,0:T(8,128)(2,1)} %bitcast.233, f32[4,8,8,128]{3,2,1,0:T(8,128)} %reshape.1649.table_ref, bf16[2,1568,2048]{2,1,0:T(8,128)(2,1)} %pool_rois.5.refs_0_), custom_call_target="tpu_custom_call", output_to_operand_aliasing={{}: (4, {})} | custom-call | flops 9395240960 | bytes 83886080 | tf_op jit(solution)/shard_map/pool_rois/pallas_call | solution.py:166
  230.7 0.6 pad_add_fusion.3.pick_ref
  231.3 0.6 convert_reduce_fusion.1
  232.0 20.6 %pool_rois.7.pooled_ref = bf16[2,1568,2048]{2,1,0:T(8,128)(2,1)} custom-call(s32[2]{0:T(128)} %pad_add_fusion.3.pick_ref, s32[544]{0:T(1024)} %reshape.1648.span_ref, bf16[4,3888,128]{2,1,0:T(8,128)(2,1)} %bitcast.234, f32[4,8,8,128]{3,2,1,0:T(8,128)} %reshape.1649.table_ref, bf16[2,1568,2048]{2,1,0:T(8,128)(2,1)} %pool_rois.6.refs_0_), custom_call_target="tpu_custom_call", output_to_operand_aliasing={{}: (4, {})} | custom-call | flops 9395240960 | bytes 83886080 | tf_op jit(solution)/shard_map/pool_rois/pallas_call | solution.py:166
  252.6 41.0 %update_first.1 = (f32[2,1568,1024]{2,1,0:T(8,128)}, f32[2,1568,1024]{2,1,0:T(8,128)}, f32[2,1568,1024]{2,1,0:T(8,128)}) custom-call(bf16[2,1568,2048]{2,1,0:T(8,128)(2,1)} %pool_rois.7.pooled_ref, bf16[2,2048,1024]{2,1,0:T(8,128)(2,1)} %get-tuple-element.41.back_ref, f32[2,1568,1024]{2,1,0:T(8,128)} %w_ref.1, f32[2,1568,1024]{2,1,0:T(8,128)} %m_ref.1, ...), custom_call_target="tpu_custom_call" | custom-call | flops 13153337344 | bytes 98304000 | tf_op jit(solution)/shard_map/update_first/pallas_call | solution.py:283
  293.6 0.6 broadcast_in_dim.133.count_ref
  294.3 1.4 copy-done.3
  295.7 1.2 copy-done.5
  297.0 5.7 %update_small.1 = (f32[2,128,1024]{2,1,0:T(8,128)}, f32[2,128,1024]{2,1,0:T(8,128)}, f32[2,128,1024]{2,1,0:T(8,128)}, f32[401,2,128]{2,1,0:T(2,128)}, f32[401,2,...) custom-call(f32[2,128,1536]{2,1,0:T(8,128)S(1)} %copy-done.3, ...), custom_call_target="tpu_custom_call" | custom-call | tf_op jit(solution)/shard_map/update_small/pallas_call | solution.py:724
  302.6 0.5 slice_bitcast_fusion.2
  (174 shorter events, 6.2 us)
Async XLA Ops:
  7.2 52.2 %all-gather.5.cloned.1.call-start = ((), (), s32[]{:S(2)}) async-start(), calls=%async_computation.1 | async-start | bytes 7077888 | tf_op jit(solution)/shard_map/all_gather | solution.py:755
  8.5 2.4 copy-start.11
  8.5 2.4 copy-start.14
  9.9 7.5 %copy-start.10 = (f32[1,32,16,16]{1,3,2,0:T(8,128)S(1)}, f32[1,32,16,16]{1,3,2,0:T(8,128)}, u32[]{:S(2)}) copy-start(f32[1,32,16,16]{1,3,2,0:T(8,128)} %param.20) | copy-start | bytes 98308
  9.9 7.7 %copy-start.12 = (f32[1,32,8,8]{1,3,2,0:T(8,128)S(1)}, f32[1,32,8,8]{1,3,2,0:T(8,128)}, u32[]{:S(2)}) copy-start(f32[1,32,8,8]{1,3,2,0:T(8,128)} %param.21) | copy-start | bytes 24580
  9.9 7.8 %copy-start.8 = (f32[1,32,64,64]{3,2,1,0:T(8,128)S(1)}, f32[1,32,64,64]{3,2,1,0:T(8,128)}, u32[]{:S(2)}) copy-start(f32[1,32,64,64]{3,2,1,0:T(8,128)} %param.18) | copy-start | bytes 1572868
  9.9 7.8 %copy-start.9 = (f32[1,32,32,32]{3,2,1,0:T(8,128)S(1)}, f32[1,32,32,32]{3,2,1,0:T(8,128)}, u32[]{:S(2)}) copy-start(f32[1,32,32,32]{3,2,1,0:T(8,128)} %param.19) | copy-start | bytes 393220
  10.9 170.7 %all-gather.9.cloned.1.call-start = ((), (), s32[]{:S(2)}) async-start(), calls=%async_computation.4 | async-start | bytes 4976640 | tf_op jit(solution)/shard_map/all_gather | solution.py:762
  17.9 0.7 copy-start.15
  45.9 13.7 %copy-start.16 = (s32[2,1,512]{2,1,0:T(1,128)S(1)}, s32[2,1,512]{2,1,0:T(1,128)}, u32[]{:S(2)}) copy-start(s32[2,1,512]{2,1,0:T(1,128)} %param.24) | copy-start | bytes 12292
  46.0 13.7 %copy-start.13 = (f32[2,1,512,4]{2,3,1,0:T(4,128)S(1)}, f32[2,1,512,4]{2,3,1,0:T(4,128)}, u32[]{:S(2)}) copy-start(f32[2,1,512,4]{2,3,1,0:T(4,128)} %param.26) | copy-start | bytes 49156
  59.4 171.3 %reduce-scatter.2.cloned.1.call-start = ((), (), s32[]{:S(2)}) async-start(), calls=%async_computation.2 | async-start | bytes 1966080 | tf_op jit(solution)/shard_map/reduce_scatter | solution.py:771
  62.1 2.2 copy-start
  181.3 112.3 %all-gather.7.cloned.1.call-start = ((), (), s32[]{:S(2)}) async-start(), calls=%async_computation.3 | async-start | bytes 1966080 | tf_op jit(solution)/shard_map/all_gather | solution.py:781
  252.6 41.7 %copy-start.1 = (f32[2,128,1024]{2,1,0:T(8,128)S(1)}, f32[2,128,1024]{2,1,0:T(8,128)}, u32[]{:S(2)}) copy-start(f32[2,128,1024]{2,1,0:T(8,128)} %refs_0_.1) | copy-start | bytes 3145732
  252.6 41.7 %copy-start.2 = (f32[2,128,401]{1,0,2:T(2,128)S(1)}, f32[2,128,401]{1,0,2:T(2,128)}, u32[]{:S(2)}) copy-start(f32[2,128,401]{1,0,2:T(2,128)} %param.33) | copy-start | bytes 1231876
  252.6 41.7 %copy-start.4 = (f32[2,128,1024]{2,1,0:T(8,128)S(1)}, f32[2,128,1024]{2,1,0:T(8,128)}, u32[]{:S(2)}) copy-start(f32[2,128,1024]{2,1,0:T(8,128)} %refs_1_.1) | copy-start | bytes 3145732
  252.6 41.7 %copy-start.6 = (f32[2,128,401]{1,0,2:T(2,128)S(1)}, f32[2,128,401]{1,0,2:T(2,128)}, u32[]{:S(2)}) copy-start(f32[2,128,401]{1,0,2:T(2,128)} %param.34) | copy-start | bytes 1231876
  252.6 41.7 %copy-start.7 = (f32[2,128,401]{1,0,2:T(2,128)S(1)}, f32[2,128,401]{1,0,2:T(2,128)}, u32[]{:S(2)}) copy-start(f32[2,128,401]{1,0,2:T(2,128)} %param.35) | copy-start | bytes 1231876
  294.3 1.4 copy-start.3
  295.7 1.2 copy-start.5
Sparse Core Ops, SparseCore 0:
  11.0 48.2 all-gather.4
  61.5 92.2 all-gather.8
  181.4 33.5 reduce-scatter.1
  230.9 35.8 all-gather.6

commit v4 on v3

--- a/solution.py
+++ b/solution.py
@@ -542,6 +542,7 @@
         for value in (back_p2, back_z, losses.astype(jnp.bfloat16)):
             kept[p, me, :, at : at + value.shape[1]] = value
             at += value.shape[1]
+        advance_kept(p, 0, 0)
         for owner in range(parts):
             split[p, 0, owner] = hid1[:, owner * span : (owner + 1) * span]
             split[p, 1, owner] = hid2[:, owner * span : (owner + 1) * span]
@@ -576,6 +577,7 @@
         if d == 0:
             for p in range(2):
                 advance(p, level, at)
+                advance_kept(p, 0, at)
         else:
 
             def do(image, up):
@@ -591,12 +593,6 @@
                 enter(d)
             elif 0 < at < bits:
                 go_on(d, at)
-        if tick % 2 and tick // 2 < bits:
-            for p in range(2):
-                advance_kept(p, 0, tick // 2)
-    for at in range((images + bits - 1) // 2, bits):
-        for p in range(2):
-            advance_kept(p, 0, at)
 
     loss = jnp.zeros((1, 1), jnp.float32)
     for p in range(2):

time: 316 us -> 305 us (0.965)
  Pallas kernels: 249 us -> 239 us
    pallas_call x1, Pallas kernels: 117 us -> 107 us  [head_step(): pl.pallas_call(partial(head_kernel, images, parts, mine), out_shape=[jax....]
  transfers between devices with their start and end apart: 4 -> 4, of which waited for: 1 -> 1; matrix products, arithmetic and copies ran while one was open for 11% -> 11% of each run, Pallas kernels for 79% -> 78%
where the time goes in v4:
time: 305 us; the launch traced here: 301 us
  Pallas kernels  239 us (78%)
  local copies, waits for them, and re-layouts  15.6 us (5%)
  between operations  15.6 us (5%)
  other arithmetic  15.1 us (5%)
  matrix products  12.3 us (4%)
    pallas_call x1, Pallas kernels, head_step(): pl.pallas_call(partial(head_kernel, images, parts, mine), out_shape=[jax....  107 us
    pallas_call x4, Pallas kernels, pool(): pl.pallas_call(partial(pool_kernel, channels, side, groups, len(out_shape...  85.7 us
    pallas_call x1, Pallas kernels, update_first(): pl.pallas_call(update_kernel, out_shape=[jax.ShapeDtypeStruct(weight.shap...  40.8 us
    dot_general x1, matrix products, per_device(): lax.dot_general(own, w1, (((1,), (1,)), ((0,), (0,))), preferred_element_...  11.9 us
  transfers between devices with their start and end apart: 4, of which 1 were waited for; matrix products, arithmetic and copies ran while one was open for 11% of the time, Pallas kernels for 78%

profile of v4, /device:TPU:0, one launch (start us, length us, event | category | flops | bytes accessed | tf_op | source)
XLA Modules:
  0.0 300.6 jit_solution(7556205982031415288)
XLA Ops:
  7.2 1.3 convert.24
  8.5 1.2 convert.25
  9.7 0.2 copy.178
  9.9 0.9 fusion.10
  11.0 0.4 convert_reduce_fusion
  11.5 0.5 fusion.8
  12.0 0.1 minimum_reduce_fusion.7
  12.3 0.1 reduce_min.187
  12.4 0.1 reduce_min.190
  12.6 0.1 reduce_min.196
  12.8 0.1 reduce_min.202
  13.0 0.1 reduce_min.205
  13.2 0.1 reduce_min.211
  13.4 0.1 reduce_min.217
  13.6 0.1 reduce_max.203
  13.7 0.1 reduce_max.209
  13.9 0.1 reduce_max.212
  14.1 0.1 reduce_max.218
  14.3 0.1 reduce_max.224
  14.5 0.1 reduce_max.227
  14.7 0.1 reduce_max.233
  15.5 0.6 reshape.1645.span_ref
  16.7 0.7 reshape.1646.table_ref
  17.4 0.2 copy.225
  17.6 0.1 copy.226
  17.7 0.1 select_maximum_fusion
  17.9 0.4 copy.176
  18.3 0.3 copy-done.15
  18.5 0.6 fusion.45
  19.2 0.6 pad_add_fusion.pick_ref
  19.8 0.3 reduce-precision_convert_fusion
  20.1 1.5 pad_maximum_fusion.1.feat_ref
  21.6 0.3 reduce-precision_convert_fusion.1
  21.9 1.5 pad_maximum_fusion
  23.4 22.0 %pool_rois.4 = (bf16[2,1568,2048]{2,1,0:T(8,128)(2,1)}, bf16[2,1568,512]{2,1,0:T(8,128)(2,1)}) custom-call(s32[2]{0:T(128)} %pad_add_fusion.pick_ref, s32[136]{0:T(256)} %reshape.1645.span_ref, bf16[1,3840,128]{2,1,0:T(8,128)(2,1)} %pad_maximum_fusion.1.feat_ref, f32[1,8,8,128]{3,2,1,0:T(8,128)} %reshape.1646.table_ref), custom_call_target="tpu_custom_call" | custom-call | flops 9395240960 | bytes 83886080 | tf_op jit(solution)/shard_map/pool_rois/pallas_call | solution.py:166
  45.4 11.9 %fusion.part_ref = f32[2,512,1024]{2,1,0:T(8,128)} fusion(bf16[2,1568,512]{2,1,0:T(8,128)(2,1)} %get-tuple-element.33, f32[2,1568,1024]{2,1,0:T(8,128)} %w_ref.1), kind=kOutput, calls=%fused_computation | convolution fusion | flops 3291545600 | bytes 20250624 | tf_op jit(solution)/shard_map/dot_general | solution.py:756
  57.3 2.1 all-gather.5.cloned.1.call-done.weight_ref
  59.4 0.2 reduce-scatter.2.cloned.1.call-start
  59.7 0.3 fusion.16
  60.1 0.1 copy.191
  60.9 0.6 pad_add_fusion.2.pick_ref
  61.5 0.6 pad_add_fusion.1.pick_ref
  62.1 2.2 copy-done
  64.2 107.0 %head_step.1 = (bf16[2,2048,1024]{2,1,0:T(8,128)(2,1)}, f32[2,128,1536]{2,1,0:T(8,128)}) custom-call(f32[2,512,1024]{2,1,0:T(8,128)S(1)} %copy-done, bf16[2,1024,1536]{2,1,0:T(8,128)(2,1)} %all-gather.5.cloned.1.call-done.weight_ref, f32[2,64,128]{2,1,0:T(8,128)S(1)} %pad.25.box_ref, f32[8,128]{1,0:T(8,128)S(1)} %broadcast_in_dim.127.count_ref), custom_call_target="tpu_custom_call" | custom-call | flops 1610612736 | bytes 104857600 | tf_op jit(solution)/shard_map/head_step/pallas_call | solution.py:657
  171.3 0.3 all-gather.7.cloned.1.call-start
  171.6 0.8 slice.89
  172.5 0.2 minimum_reduce_fusion
  175.3 0.1 copy.199
  176.1 0.8 reshape.1649.table_ref
  177.0 0.1 copy.197
  177.1 0.1 copy.198
  177.2 0.1 copy.195
  177.5 0.7 reshape.1648.span_ref
  178.2 20.5 %pool_rois.5.refs_0_ = bf16[2,1568,2048]{2,1,0:T(8,128)(2,1)} custom-call(s32[2]{0:T(128)} %pad_add_fusion.2.pick_ref, s32[544]{0:T(1024)} %reshape.1648.span_ref, bf16[4,3888,128]{2,1,0:T(8,128)(2,1)} %bitcast.232, f32[4,8,8,128]{3,2,1,0:T(8,128)} %reshape.1649.table_ref, ...), custom_call_target="tpu_custom_call", output_to_operand_aliasing={{}: (4, {})} | custom-call | flops 9395240960 | bytes 83886080 | tf_op jit(solution)/shard_map/pool_rois/pallas_call | solution.py:166
  198.7 21.4 %pool_rois.6.refs_0_ = bf16[2,1568,2048]{2,1,0:T(8,128)(2,1)} custom-call(s32[2]{0:T(128)} %pad_add_fusion.1.pick_ref, s32[544]{0:T(1024)} %reshape.1648.span_ref, bf16[4,3888,128]{2,1,0:T(8,128)(2,1)} %bitcast.233, f32[4,8,8,128]{3,2,1,0:T(8,128)} %reshape.1649.table_ref, bf16[2,1568,2048]{2,1,0:T(8,128)(2,1)} %pool_rois.5.refs_0_), custom_call_target="tpu_custom_call", output_to_operand_aliasing={{}: (4, {})} | custom-call | flops 9395240960 | bytes 83886080 | tf_op jit(solution)/shard_map/pool_rois/pallas_call | solution.py:166
  220.1 0.6 pad_add_fusion.3.pick_ref
  220.7 0.6 convert_reduce_fusion.1
  221.3 21.9 %pool_rois.7.pooled_ref = bf16[2,1568,2048]{2,1,0:T(8,128)(2,1)} custom-call(s32[2]{0:T(128)} %pad_add_fusion.3.pick_ref, s32[544]{0:T(1024)} %reshape.1648.span_ref, bf16[4,3888,128]{2,1,0:T(8,128)(2,1)} %bitcast.234, f32[4,8,8,128]{3,2,1,0:T(8,128)} %reshape.1649.table_ref, bf16[2,1568,2048]{2,1,0:T(8,128)(2,1)} %pool_rois.6.refs_0_), custom_call_target="tpu_custom_call", output_to_operand_aliasing={{}: (4, {})} | custom-call | flops 9395240960 | bytes 83886080 | tf_op jit(solution)/shard_map/pool_rois/pallas_call | solution.py:166
  243.2 40.8 %update_first.1 = (f32[2,1568,1024]{2,1,0:T(8,128)}, f32[2,1568,1024]{2,1,0:T(8,128)}, f32[2,1568,1024]{2,1,0:T(8,128)}) custom-call(bf16[2,1568,2048]{2,1,0:T(8,128)(2,1)} %pool_rois.7.pooled_ref, bf16[2,2048,1024]{2,1,0:T(8,128)(2,1)} %get-tuple-element.41.back_ref, f32[2,1568,1024]{2,1,0:T(8,128)} %w_ref.1, f32[2,1568,1024]{2,1,0:T(8,128)} %m_ref.1, ...), custom_call_target="tpu_custom_call" | custom-call | flops 13153337344 | bytes 98304000 | tf_op jit(solution)/shard_map/update_first/pallas_call | solution.py:283
  284.0 0.6 broadcast_in_dim.133.count_ref
  284.7 1.4 copy-done.3
  286.1 1.2 copy-done.5
  287.3 5.7 %update_small.1 = (f32[2,128,1024]{2,1,0:T(8,128)}, f32[2,128,1024]{2,1,0:T(8,128)}, f32[2,128,1024]{2,1,0:T(8,128)}, f32[401,2,128]{2,1,0:T(2,128)}, f32[401,2,...) custom-call(f32[2,128,1536]{2,1,0:T(8,128)S(1)} %copy-done.3, ...), custom_call_target="tpu_custom_call" | custom-call | tf_op jit(solution)/shard_map/update_small/pallas_call | solution.py:720
  293.0 0.5 slice_bitcast_fusion.2
  (174 shorter events, 6.2 us)
Async XLA Ops:
  7.2 52.2 %all-gather.5.cloned.1.call-start = ((), (), s32[]{:S(2)}) async-start(), calls=%async_computation.1 | async-start | bytes 7077888 | tf_op jit(solution)/shard_map/all_gather | solution.py:751
  8.5 2.4 copy-start.11
  8.5 2.4 copy-start.14
  9.9 7.5 %copy-start.10 = (f32[1,32,16,16]{1,3,2,0:T(8,128)S(1)}, f32[1,32,16,16]{1,3,2,0:T(8,128)}, u32[]{:S(2)}) copy-start(f32[1,32,16,16]{1,3,2,0:T(8,128)} %param.20) | copy-start | bytes 98308
  9.9 7.7 %copy-start.12 = (f32[1,32,8,8]{1,3,2,0:T(8,128)S(1)}, f32[1,32,8,8]{1,3,2,0:T(8,128)}, u32[]{:S(2)}) copy-start(f32[1,32,8,8]{1,3,2,0:T(8,128)} %param.21) | copy-start | bytes 24580
  9.9 7.8 %copy-start.8 = (f32[1,32,64,64]{3,2,1,0:T(8,128)S(1)}, f32[1,32,64,64]{3,2,1,0:T(8,128)}, u32[]{:S(2)}) copy-start(f32[1,32,64,64]{3,2,1,0:T(8,128)} %param.18) | copy-start | bytes 1572868
  9.9 7.8 %copy-start.9 = (f32[1,32,32,32]{3,2,1,0:T(8,128)S(1)}, f32[1,32,32,32]{3,2,1,0:T(8,128)}, u32[]{:S(2)}) copy-start(f32[1,32,32,32]{3,2,1,0:T(8,128)} %param.19) | copy-start | bytes 393220
  10.9 160.7 %all-gather.9.cloned.1.call-start = ((), (), s32[]{:S(2)}) async-start(), calls=%async_computation.4 | async-start | bytes 4976640 | tf_op jit(solution)/shard_map/all_gather | solution.py:758
  17.9 0.7 copy-start.15
  45.4 14.2 %copy-start.16 = (s32[2,1,512]{2,1,0:T(1,128)S(1)}, s32[2,1,512]{2,1,0:T(1,128)}, u32[]{:S(2)}) copy-start(s32[2,1,512]{2,1,0:T(1,128)} %param.24) | copy-start | bytes 12292
  45.4 14.3 %copy-start.13 = (f32[2,1,512,4]{2,3,1,0:T(4,128)S(1)}, f32[2,1,512,4]{2,3,1,0:T(4,128)}, u32[]{:S(2)}) copy-start(f32[2,1,512,4]{2,3,1,0:T(4,128)} %param.26) | copy-start | bytes 49156
  59.4 160.7 %reduce-scatter.2.cloned.1.call-start = ((), (), s32[]{:S(2)}) async-start(), calls=%async_computation.2 | async-start | bytes 1966080 | tf_op jit(solution)/shard_map/reduce_scatter | solution.py:767
  62.1 2.2 copy-start
  171.3 112.7 %all-gather.7.cloned.1.call-start = ((), (), s32[]{:S(2)}) async-start(), calls=%async_computation.3 | async-start | bytes 1966080 | tf_op jit(solution)/shard_map/all_gather | solution.py:777
  243.2 41.5 %copy-start.1 = (f32[2,128,1024]{2,1,0:T(8,128)S(1)}, f32[2,128,1024]{2,1,0:T(8,128)}, u32[]{:S(2)}) copy-start(f32[2,128,1024]{2,1,0:T(8,128)} %refs_0_.1) | copy-start | bytes 3145732
  243.2 41.5 %copy-start.2 = (f32[2,128,401]{1,0,2:T(2,128)S(1)}, f32[2,128,401]{1,0,2:T(2,128)}, u32[]{:S(2)}) copy-start(f32[2,128,401]{1,0,2:T(2,128)} %param.33) | copy-start | bytes 1231876
  243.2 41.5 %copy-start.4 = (f32[2,128,1024]{2,1,0:T(8,128)S(1)}, f32[2,128,1024]{2,1,0:T(8,128)}, u32[]{:S(2)}) copy-start(f32[2,128,1024]{2,1,0:T(8,128)} %refs_1_.1) | copy-start | bytes 3145732
  243.2 41.5 %copy-start.6 = (f32[2,128,401]{1,0,2:T(2,128)S(1)}, f32[2,128,401]{1,0,2:T(2,128)}, u32[]{:S(2)}) copy-start(f32[2,128,401]{1,0,2:T(2,128)} %param.34) | copy-start | bytes 1231876
  243.2 41.5 %copy-start.7 = (f32[2,128,401]{1,0,2:T(2,128)S(1)}, f32[2,128,401]{1,0,2:T(2,128)}, u32[]{:S(2)}) copy-start(f32[2,128,401]{1,0,2:T(2,128)} %param.35) | copy-start | bytes 1231876
  284.7 1.4 copy-start.3
  286.1 1.2 copy-start.5
Sparse Core Ops, SparseCore 0:
  11.0 48.2 all-gather.4
  61.5 91.9 all-gather.8
  171.4 33.6 reduce-scatter.1
  220.2 35.4 all-gather.6

commit v5 on v4

--- a/solution.py
+++ b/solution.py
@@ -532,16 +532,14 @@
 
         advance(p, level, 0, own.at[p])
         pltpu.make_async_copy(own.at[p], rows(p, level, 0), own_sem.at[p]).start()
-        place = lax.broadcasted_iota(jnp.int32, (mine, LANES), 1)
-        losses = jnp.zeros((mine, LANES), jnp.float32)
+        place = lax.broadcasted_iota(jnp.int32, back_z.shape, 1)
+        shown = back_z.astype(jnp.float32)
         for k in range(3):
             near = loss.astype(jnp.bfloat16).astype(jnp.float32)
-            losses = jnp.where(place == k, near, losses)
+            shown = jnp.where(place == back_z.shape[1] - 1 - k, near, shown)
             loss = loss - near
-        at = 0
-        for value in (back_p2, back_z, losses.astype(jnp.bfloat16)):
-            kept[p, me, :, at : at + value.shape[1]] = value
-            at += value.shape[1]
+        kept[p, me, :, :hidden] = back_p2
+        kept[p, me, :, hidden:] = shown.astype(jnp.bfloat16)
         advance_kept(p, 0, 0)
         for owner in range(parts):
             split[p, 0, owner] = hid1[:, owner * span : (owner + 1) * span]
@@ -608,7 +606,9 @@
             grad_ref[p, :, start:stop] = lax.dot_general(
                 left, slopes[:, start:stop], down, preferred_element_type=jnp.float32
             )
-        loss += jnp.sum(slopes[:, grad_ref.shape[2] :].astype(jnp.float32), keepdims=True)
+        ends = slopes[:, grad_ref.shape[2] - LANES :].astype(jnp.float32)
+        place = lax.broadcasted_iota(jnp.int32, ends.shape, 1)
+        loss += jnp.sum(jnp.where(place >= LANES - 3, ends, 0.0), keepdims=True)
     corner = grad_ref[0, 0:8, grad_ref.shape[2] - LANES :]
     place = [lax.broadcasted_iota(jnp.int32, corner.shape, k) for k in range(2)]
     corner = jnp.where((place[0] == 0) & (place[1] == LANES - 1), loss, corner)
@@ -669,7 +669,7 @@
             pltpu.VMEM((images, 8, LANES), jnp.float32),
             pltpu.VMEM((passes, 2, parts, mine, span), low),
             pltpu.VMEM((passes, 2, parts, mine, span), low),
-            pltpu.VMEM((passes, parts, mine, hidden + outs + LANES), low),
+            pltpu.VMEM((passes, parts, mine, hidden + outs), low),
             dma((passes, parts)),
             dma((passes, parts)),
             dma((passes, images, parts)),

time: 305 us -> 306 us (level)
  no operation moved by 1% of the time
where the time goes in v5:
time: 306 us; the launch traced here: 301 us
  Pallas kernels  240 us (78%)
  local copies, waits for them, and re-layouts  15.6 us (5%)
  between operations  15.6 us (5%)
  other arithmetic  15.1 us (5%)
  matrix products  12.3 us (4%)
    pallas_call x1, Pallas kernels, head_step(): pl.pallas_call(partial(head_kernel, images, parts, mine), out_shape=[jax....  107 us
    pallas_call x4, Pallas kernels, pool(): pl.pallas_call(partial(pool_kernel, channels, side, groups, len(out_shape...  86.2 us
    pallas_call x1, Pallas kernels, update_first(): pl.pallas_call(update_kernel, out_shape=[jax.ShapeDtypeStruct(weight.shap...  40.8 us
    dot_general x1, matrix products, per_device(): lax.dot_general(own, w1, (((1,), (1,)), ((0,), (0,))), preferred_element_...  11.9 us
  transfers between devices with their start and end apart: 4, of which 1 were waited for; matrix products, arithmetic and copies ran while one was open for 11% of the time, Pallas kernels for 78%

profile of v5, /device:TPU:0, one launch (start us, length us, event | category | flops | bytes accessed | tf_op | source)
XLA Modules:
  0.0 301.2 jit_solution(10548275060978966151)
XLA Ops:
  7.2 1.3 convert.24
  8.5 1.2 convert.25
  9.7 0.2 copy.178
  9.9 0.9 fusion.10
  11.0 0.4 convert_reduce_fusion
  11.5 0.5 fusion.8
  12.0 0.1 minimum_reduce_fusion.7
  12.3 0.1 reduce_min.187
  12.4 0.1 reduce_min.190
  12.6 0.1 reduce_min.196
  12.8 0.1 reduce_min.202
  13.0 0.1 reduce_min.205
  13.2 0.1 reduce_min.211
  13.4 0.1 reduce_min.217
  13.6 0.1 reduce_max.203
  13.7 0.1 reduce_max.209
  13.9 0.1 reduce_max.212
  14.1 0.1 reduce_max.218
  14.3 0.1 reduce_max.224
  14.5 0.1 reduce_max.227
  14.7 0.1 reduce_max.233
  15.5 0.6 reshape.1645.span_ref
  16.7 0.7 reshape.1646.table_ref
  17.4 0.2 copy.225
  17.6 0.1 copy.226
  17.7 0.1 select_maximum_fusion
  17.9 0.4 copy.176
  18.3 0.3 copy-done.15
  18.5 0.6 fusion.45
  19.2 0.6 pad_add_fusion.pick_ref
  19.8 0.3 reduce-precision_convert_fusion
  20.1 1.5 pad_maximum_fusion.1.feat_ref
  21.6 0.3 reduce-precision_convert_fusion.1
  21.9 1.5 pad_maximum_fusion
  23.4 21.8 %pool_rois.4 = (bf16[2,1568,2048]{2,1,0:T(8,128)(2,1)}, bf16[2,1568,512]{2,1,0:T(8,128)(2,1)}) custom-call(s32[2]{0:T(128)} %pad_add_fusion.pick_ref, s32[136]{0:T(256)} %reshape.1645.span_ref, bf16[1,3840,128]{2,1,0:T(8,128)(2,1)} %pad_maximum_fusion.1.feat_ref, f32[1,8,8,128]{3,2,1,0:T(8,128)} %reshape.1646.table_ref), custom_call_target="tpu_custom_call" | custom-call | flops 9395240960 | bytes 83886080 | tf_op jit(solution)/shard_map/pool_rois/pallas_call | solution.py:166
  45.3 11.9 %fusion.part_ref = f32[2,512,1024]{2,1,0:T(8,128)} fusion(bf16[2,1568,512]{2,1,0:T(8,128)(2,1)} %get-tuple-element.33, f32[2,1568,1024]{2,1,0:T(8,128)} %w_ref.1), kind=kOutput, calls=%fused_computation | convolution fusion | flops 3291545600 | bytes 20250624 | tf_op jit(solution)/shard_map/dot_general | solution.py:756
  57.1 2.2 all-gather.5.cloned.1.call-done.weight_ref
  59.4 0.2 reduce-scatter.2.cloned.1.call-start
  59.7 0.3 fusion.16
  60.1 0.1 copy.191
  60.9 0.6 pad_add_fusion.2.pick_ref
  61.5 0.6 pad_add_fusion.1.pick_ref
  62.1 2.2 copy-done
  64.2 107.0 %head_step.1 = (bf16[2,2048,1024]{2,1,0:T(8,128)(2,1)}, f32[2,128,1536]{2,1,0:T(8,128)}) custom-call(f32[2,512,1024]{2,1,0:T(8,128)S(1)} %copy-done, bf16[2,1024,1536]{2,1,0:T(8,128)(2,1)} %all-gather.5.cloned.1.call-done.weight_ref, f32[2,64,128]{2,1,0:T(8,128)S(1)} %pad.25.box_ref, f32[8,128]{1,0:T(8,128)S(1)} %broadcast_in_dim.127.count_ref), custom_call_target="tpu_custom_call" | custom-call | flops 1610612736 | bytes 104857600 | tf_op jit(solution)/shard_map/head_step/pallas_call | solution.py:657
  171.2 0.3 all-gather.7.cloned.1.call-start
  171.5 0.8 slice.89
  172.4 0.2 minimum_reduce_fusion
  175.3 0.1 copy.199
  176.1 0.8 reshape.1649.table_ref
  177.0 0.1 copy.198
  177.2 0.1 copy.195
  177.3 0.1 copy.196
  177.4 0.7 reshape.1648.span_ref
  178.1 21.9 %pool_rois.5.refs_0_ = bf16[2,1568,2048]{2,1,0:T(8,128)(2,1)} custom-call(s32[2]{0:T(128)} %pad_add_fusion.2.pick_ref, s32[544]{0:T(1024)} %reshape.1648.span_ref, bf16[4,3888,128]{2,1,0:T(8,128)(2,1)} %bitcast.232, f32[4,8,8,128]{3,2,1,0:T(8,128)} %reshape.1649.table_ref, ...), custom_call_target="tpu_custom_call", output_to_operand_aliasing={{}: (4, {})} | custom-call | flops 9395240960 | bytes 83886080 | tf_op jit(solution)/shard_map/pool_rois/pallas_call | solution.py:166
  200.0 21.6 %pool_rois.6.refs_0_ = bf16[2,1568,2048]{2,1,0:T(8,128)(2,1)} custom-call(s32[2]{0:T(128)} %pad_add_fusion.1.pick_ref, s32[544]{0:T(1024)} %reshape.1648.span_ref, bf16[4,3888,128]{2,1,0:T(8,128)(2,1)} %bitcast.233, f32[4,8,8,128]{3,2,1,0:T(8,128)} %reshape.1649.table_ref, bf16[2,1568,2048]{2,1,0:T(8,128)(2,1)} %pool_rois.5.refs_0_), custom_call_target="tpu_custom_call", output_to_operand_aliasing={{}: (4, {})} | custom-call | flops 9395240960 | bytes 83886080 | tf_op jit(solution)/shard_map/pool_rois/pallas_call | solution.py:166
  221.6 0.6 pad_add_fusion.3.pick_ref
  222.2 0.6 convert_reduce_fusion.1
  222.8 20.9 %pool_rois.7.pooled_ref = bf16[2,1568,2048]{2,1,0:T(8,128)(2,1)} custom-call(s32[2]{0:T(128)} %pad_add_fusion.3.pick_ref, s32[544]{0:T(1024)} %reshape.1648.span_ref, bf16[4,3888,128]{2,1,0:T(8,128)(2,1)} %bitcast.234, f32[4,8,8,128]{3,2,1,0:T(8,128)} %reshape.1649.table_ref, bf16[2,1568,2048]{2,1,0:T(8,128)(2,1)} %pool_rois.6.refs_0_), custom_call_target="tpu_custom_call", output_to_operand_aliasing={{}: (4, {})} | custom-call | flops 9395240960 | bytes 83886080 | tf_op jit(solution)/shard_map/pool_rois/pallas_call | solution.py:166
  243.8 40.8 %update_first.1 = (f32[2,1568,1024]{2,1,0:T(8,128)}, f32[2,1568,1024]{2,1,0:T(8,128)}, f32[2,1568,1024]{2,1,0:T(8,128)}) custom-call(bf16[2,1568,2048]{2,1,0:T(8,128)(2,1)} %pool_rois.7.pooled_ref, bf16[2,2048,1024]{2,1,0:T(8,128)(2,1)} %get-tuple-element.41.back_ref, f32[2,1568,1024]{2,1,0:T(8,128)} %w_ref.1, f32[2,1568,1024]{2,1,0:T(8,128)} %m_ref.1, ...), custom_call_target="tpu_custom_call" | custom-call | flops 13153337344 | bytes 98304000 | tf_op jit(solution)/shard_map/update_first/pallas_call | solution.py:283
  284.6 0.6 broadcast_in_dim.133.count_ref
  285.3 1.4 copy-done.3
  286.7 1.2 copy-done.5
  287.9 5.7 %update_small.1 = (f32[2,128,1024]{2,1,0:T(8,128)}, f32[2,128,1024]{2,1,0:T(8,128)}, f32[2,128,1024]{2,1,0:T(8,128)}, f32[401,2,128]{2,1,0:T(2,128)}, f32[401,2,...) custom-call(f32[2,128,1536]{2,1,0:T(8,128)S(1)} %copy-done.3, ...), custom_call_target="tpu_custom_call" | custom-call | tf_op jit(solution)/shard_map/update_small/pallas_call | solution.py:720
  293.6 0.5 slice_bitcast_fusion.2
  (174 shorter events, 6.2 us)
Async XLA Ops:
  7.2 52.2 %all-gather.5.cloned.1.call-start = ((), (), s32[]{:S(2)}) async-start(), calls=%async_computation.1 | async-start | bytes 7077888 | tf_op jit(solution)/shard_map/all_gather | solution.py:751
  8.5 2.4 copy-start.11
  8.5 2.4 copy-start.14
  9.9 7.5 %copy-start.10 = (f32[1,32,16,16]{1,3,2,0:T(8,128)S(1)}, f32[1,32,16,16]{1,3,2,0:T(8,128)}, u32[]{:S(2)}) copy-start(f32[1,32,16,16]{1,3,2,0:T(8,128)} %param.20) | copy-start | bytes 98308
  9.9 7.7 %copy-start.12 = (f32[1,32,8,8]{1,3,2,0:T(8,128)S(1)}, f32[1,32,8,8]{1,3,2,0:T(8,128)}, u32[]{:S(2)}) copy-start(f32[1,32,8,8]{1,3,2,0:T(8,128)} %param.21) | copy-start | bytes 24580
  9.9 7.8 %copy-start.8 = (f32[1,32,64,64]{3,2,1,0:T(8,128)S(1)}, f32[1,32,64,64]{3,2,1,0:T(8,128)}, u32[]{:S(2)}) copy-start(f32[1,32,64,64]{3,2,1,0:T(8,128)} %param.18) | copy-start | bytes 1572868
  9.9 7.8 %copy-start.9 = (f32[1,32,32,32]{3,2,1,0:T(8,128)S(1)}, f32[1,32,32,32]{3,2,1,0:T(8,128)}, u32[]{:S(2)}) copy-start(f32[1,32,32,32]{3,2,1,0:T(8,128)} %param.19) | copy-start | bytes 393220
  10.9 160.6 %all-gather.9.cloned.1.call-start = ((), (), s32[]{:S(2)}) async-start(), calls=%async_computation.4 | async-start | bytes 4976640 | tf_op jit(solution)/shard_map/all_gather | solution.py:758
  17.9 0.7 copy-start.15
  45.3 14.4 %copy-start.16 = (s32[2,1,512]{2,1,0:T(1,128)S(1)}, s32[2,1,512]{2,1,0:T(1,128)}, u32[]{:S(2)}) copy-start(s32[2,1,512]{2,1,0:T(1,128)} %param.24) | copy-start | bytes 12292
  45.3 14.4 %copy-start.13 = (f32[2,1,512,4]{2,3,1,0:T(4,128)S(1)}, f32[2,1,512,4]{2,3,1,0:T(4,128)}, u32[]{:S(2)}) copy-start(f32[2,1,512,4]{2,3,1,0:T(4,128)} %param.26) | copy-start | bytes 49156
  59.4 162.2 %reduce-scatter.2.cloned.1.call-start = ((), (), s32[]{:S(2)}) async-start(), calls=%async_computation.2 | async-start | bytes 1966080 | tf_op jit(solution)/shard_map/reduce_scatter | solution.py:767
  62.1 2.2 copy-start
  171.2 113.3 %all-gather.7.cloned.1.call-start = ((), (), s32[]{:S(2)}) async-start(), calls=%async_computation.3 | async-start | bytes 1966080 | tf_op jit(solution)/shard_map/all_gather | solution.py:777
  243.7 41.5 %copy-start.1 = (f32[2,128,1024]{2,1,0:T(8,128)S(1)}, f32[2,128,1024]{2,1,0:T(8,128)}, u32[]{:S(2)}) copy-start(f32[2,128,1024]{2,1,0:T(8,128)} %refs_0_.1) | copy-start | bytes 3145732
  243.7 41.5 %copy-start.2 = (f32[2,128,401]{1,0,2:T(2,128)S(1)}, f32[2,128,401]{1,0,2:T(2,128)}, u32[]{:S(2)}) copy-start(f32[2,128,401]{1,0,2:T(2,128)} %param.33) | copy-start | bytes 1231876
  243.7 41.5 %copy-start.4 = (f32[2,128,1024]{2,1,0:T(8,128)S(1)}, f32[2,128,1024]{2,1,0:T(8,128)}, u32[]{:S(2)}) copy-start(f32[2,128,1024]{2,1,0:T(8,128)} %refs_1_.1) | copy-start | bytes 3145732
  243.7 41.5 %copy-start.6 = (f32[2,128,401]{1,0,2:T(2,128)S(1)}, f32[2,128,401]{1,0,2:T(2,128)}, u32[]{:S(2)}) copy-start(f32[2,128,401]{1,0,2:T(2,128)} %param.34) | copy-start | bytes 1231876
  243.7 41.5 %copy-start.7 = (f32[2,128,401]{1,0,2:T(2,128)S(1)}, f32[2,128,401]{1,0,2:T(2,128)}, u32[]{:S(2)}) copy-start(f32[2,128,401]{1,0,2:T(2,128)} %param.35) | copy-start | bytes 1231876
  285.3 1.4 copy-start.3
  286.7 1.2 copy-start.5
Sparse Core Ops, SparseCore 0:
  11.0 48.2 all-gather.4
  61.5 92.2 all-gather.8
  171.4 33.4 reduce-scatter.1
  221.7 35.0 all-gather.6
